TPU v7x, 1024 devices: a whole 4x4x32 slice. The times are simulated.
1024 devices in a mesh: dia: 8 (over z_lo), sub: 32 (over y, z_hi, core), rad: 4 (over x).
Axes of the slice: x: 4, y: 4, z: 32 (z_hi: 4, z_lo: 8; z = z_hi * 8 + z_lo), core: 2. Of those that a mesh axis runs over, the one named last changes fastest.
Arguments:
- sensitivity_heat: float32 [16, 512, 8192], P('rad', 'sub', 'dia'), may hold values from -1.1 to 5.3
- stored_heat: float32 [16, 512, 8192], P('rad', 'sub', 'dia'), may hold values from -1 to 521
- friction_diagonal: float32 [16, 512, 8192], P('rad', 'sub', 'dia'), may hold values from 0.1 to 12
- stored_motions: bfloat16 [2, 3, 16, 512, 8192], P(None, None, 'rad', 'sub', 'dia'), may hold values from -5 to 5
- record_choice_table: int32 [16], P('dia'), may hold values from 0 to 1
Outputs:
- adj_temperature: float32 [16, 512, 8192], P('rad', 'sub', 'dia')
- adj_velocity: float32 [3, 16, 512, 8192], P(None, 'rad', 'sub', 'dia')
All inputs are finite; a program needn't handle non-finite values.
Results may differ from a plain program's by a relative error of at most 0.0003.
Values sent between devices are 32-bit elements; how exact they have to be, the bound alone decides.
A program may use at most 64 MiB of HBM per device.

v0:
```python
import jax
import jax.numpy as jnp
from jax import lax
from jax.sharding import PartitionSpec as P

SWEEPS = 3


def padded(block, sides, width, periodic):
    for axis, dim in sides:
        count = lax.axis_size(axis)
        forward = [(i, i + 1) for i in range(count - 1)]
        if periodic:
            forward.append((count - 1, 0))
        backward = [(target, source) for source, target in forward]
        low = lax.ppermute(
            lax.slice_in_dim(block, block.shape[dim] - width, None, axis=dim), axis, forward
        )
        high = lax.ppermute(lax.slice_in_dim(block, 0, width, axis=dim), axis, backward)
        block = jnp.concatenate([low, block, high], axis=dim)
    return block


def adjacent_slots(field):
    seamed = padded(field, (("dia", 3),), 1, True)
    faced = padded(field, (("rad", 1), ("sub", 2)), 1, False)
    upper = (faced[:, 2:, 1:-1], faced[:, 1:-1, 2:], seamed[..., 2:])
    lower = (faced[:, :-2, 1:-1], faced[:, 1:-1, :-2], seamed[..., :-2])
    return (upper, lower)


def inner_sums(first, second):
    return lax.psum((first, second), ("dia", "sub", "rad"))


def shards(sensitivity_heat, stored_heat, friction_diagonal, stored_motions, record_choice_table):
    layers, across, columns = sensitivity_heat.shape
    slots = record_choice_table.shape[0]
    per_slot = columns // slots
    column_dia = jnp.arange(columns, dtype=jnp.int32) // per_slot
    picked = jnp.where(
        column_dia[:, None] == jnp.arange(slots, dtype=jnp.int32)[None, :],
        record_choice_table[None, :],
        0,
    )
    chosen = jnp.sum(picked, axis=1)
    motion_speed = jnp.zeros((3, layers, across, columns), jnp.float32)
    for snap in range(stored_motions.shape[0]):
        motion_speed = motion_speed + jnp.where(
            (chosen == snap)[None, None, None, :], stored_motions[snap].astype(jnp.float32), 0.0
        )
    piled_quantities = jnp.concatenate(
        [sensitivity_heat[None], motion_speed * sensitivity_heat[None], stored_heat[None]], 0
    )
    upper, lower = adjacent_slots(piled_quantities)
    laplace = (
        upper[0][0]
        + lower[0][0]
        + upper[1][0]
        + lower[1][0]
        + upper[2][0]
        + lower[2][0]
        - 6.0 * sensitivity_heat
    )
    flux = upper[0][1] - lower[0][1] + (upper[1][2] - lower[1][2]) + (upper[2][3] - lower[2][3])
    advected = sensitivity_heat + 0.25 * laplace + 0.125 * flux
    source = jnp.stack([-0.5 * sensitivity_heat * (upper[c][4] - lower[c][4]) for c in range(3)], 0)
    velocity_adj = jnp.zeros_like(source)
    diagonal = 6.0 + friction_diagonal[None]
    residual = source
    for sweep in range(SWEEPS):
        scaled = residual / diagonal
        upper, lower = adjacent_slots(scaled)
        beside_all = upper[0] + lower[0] + upper[1] + lower[1] + upper[2] + lower[2]
        image = diagonal * scaled - beside_all
        alpha_num, alpha_den = inner_sums(jnp.sum(residual * scaled), jnp.sum(scaled * image))
        alpha = alpha_num / alpha_den
        velocity_adj = velocity_adj + alpha * scaled
        residual = residual - alpha * image
    return (advected + 4.0 * velocity_adj[0], velocity_adj)


def solution(mesh):
    placed = (
        P("rad", "sub", "dia"),
        P("rad", "sub", "dia"),
        P("rad", "sub", "dia"),
        P(None, None, "rad", "sub", "dia"),
        P("dia"),
    )
    return jax.shard_map(
        shards,
        mesh=mesh,
        in_specs=placed,
        out_specs=(P("rad", "sub", "dia"), P(None, "rad", "sub", "dia")),
        check_vma=False,
    )
```

profile of v0, /device:TPU:1, one launch (start us, length us, event | category | flops | bytes accessed | tf_op | source)
XLA Modules:
  0.0 656.6 jit_solution(14011969129094643622)
XLA Ops:
  3.0 4.0 collective-permute-start.1
  8.4 12.9 %collective-permute-start.4 = (f32[5,4,16,1]{3,2,1,0:T(8,128)S(1)}, f32[5,4,16,1]{3,2,1,0:T(8,128)S(1)}, u32[]{:S(2)}, u32[]{:S(2)}) collective-permute-start(f32[5,4,16,1]{3,2,1,0:T(8,128)S(1)} %get-tuple-element.24), channel_id=1, source_target_pairs={{128,0},{256,128},{384,256},{512,384},{640,512},{768,640},{896,768... | collective-permute-start | bytes 3848 | tf_op jit(solution)/shard_map/ppermute | solution.py:19
  23.5 6.1 collective-permute-start.2
  29.6 12.4 %collective-permute-start.3 = (f32[5,6,1,1024]{3,2,1,0:T(1,128)S(1)}, f32[5,6,1,1024]{3,2,1,0:T(1,128)S(1)}, u32[]{:S(2)}, u32[]{:S(2)}) collective-permute-start(f32[5,6,1,1024]{3,2,1,0:T(1,128)S(1)} %get-tuple-element.19), channel_id=1, source_target_pairs={{0,4},{4,8},{8,12},{12,16},{16,20},{20,24},{24,28},{28,32},{32,36}... | collective-permute-start | bytes 368648 | tf_op jit(solution)/shard_map/ppermute | solution.py:16
  42.8 2.9 collective-permute-done.2
  46.5 5.1 collective-permute-start.7
  54.2 3.8 collective-permute-done.6
  60.1 12.4 %collective-permute-start.9 = (f32[3,6,1,1024]{3,2,1,0:T(1,128)S(1)}, f32[3,6,1,1024]{3,2,1,0:T(1,128)S(1)}, u32[]{:S(2)}, u32[]{:S(2)}) collective-permute-start(f32[3,6,1,1024]{3,2,1,0:T(1,128)S(1)} %get-tuple-element.31), channel_id=1, source_target_pairs={{0,4},{4,8},{8,12},{12,16},{16,20},{20,24},{24,28},{28,32},{32,36}... | collective-permute-start | bytes 221192 | tf_op jit(solution)/shard_map/ppermute | solution.py:16
  72.5 13.0 %collective-permute-start.10 = (f32[3,4,16,1]{3,2,1,0:T(8,128)S(1)}, f32[3,4,16,1]{3,2,1,0:T(8,128)S(1)}, u32[]{:S(2)}, u32[]{:S(2)}) collective-permute-start(f32[3,4,16,1]{3,2,1,0:T(8,128)S(1)} %get-tuple-element.42), channel_id=1, source_target_pairs={{128,0},{256,128},{384,256},{512,384},{640,512},{768,640},{896,768... | collective-permute-start | bytes 2312 | tf_op jit(solution)/shard_map/ppermute | solution.py:19
  88.1 9.3 %collective-permute-done.11 = f32[3,4,16,1]{3,2,1,0:T(8,128)S(1)} collective-permute-done((f32[3,4,16,1]{3,2,1,0:T(8,128)S(1)}, f32[3,4,16,1]{3,2,1,0:T(8,128)S(1)}, u32[]{:S(2)}, u32[]{:S(2)}) %collective-permute-start.11) | collective-permute-done | bytes 800 | tf_op jit(solution)/shard_map/ppermute | solution.py:16
  99.7 154.0 %all-reduce.2 = (f32[]{:T(128)}, f32[]{:T(128)}) all-reduce(f32[]{:T(128)} %get-tuple-element.5, f32[]{:T(128)} %get-tuple-element.4), channel_id=1, replica_groups=mesh['dia'=8,'sub'=32,'rad'=4] {'dia','sub','rad'}, use_global_device_ids=true, to_apply=%region_2.3 | all-reduce | flops 2 | bytes 16 | tf_op jit(solution)/shard_map/psum | solution.py:33
  256.4 2.7 collective-permute-start.13
  262.7 3.8 collective-permute-done.12
  266.6 3.8 collective-permute-start.14
  270.4 10.5 %collective-permute-start.15 = (f32[3,6,1,1024]{3,2,1,0:T(1,128)S(1)}, f32[3,6,1,1024]{3,2,1,0:T(1,128)S(1)}, u32[]{:S(2)}, u32[]{:S(2)}) collective-permute-start(f32[3,6,1,1024]{3,2,1,0:T(1,128)S(1)} %get-tuple-element.29), channel_id=1, source_target_pairs={{0,4},{4,8},{8,12},{12,16},{16,20},{20,24},{24,28},{28,32},{32,36}... | collective-permute-start | bytes 221192 | tf_op jit(solution)/shard_map/ppermute | solution.py:16
  281.0 9.4 %collective-permute-start.16 = (f32[3,4,16,1]{3,2,1,0:T(8,128)S(1)}, f32[3,4,16,1]{3,2,1,0:T(8,128)S(1)}, u32[]{:S(2)}, u32[]{:S(2)}) collective-permute-start(f32[3,4,16,1]{3,2,1,0:T(8,128)S(1)} %get-tuple-element.38), channel_id=1, source_target_pairs={{128,0},{256,128},{384,256},{512,384},{640,512},{768,640},{896,768... | collective-permute-start | bytes 2312 | tf_op jit(solution)/shard_map/ppermute | solution.py:19
  292.3 10.0 %collective-permute-done.17 = f32[3,4,16,1]{3,2,1,0:T(8,128)S(1)} collective-permute-done((f32[3,4,16,1]{3,2,1,0:T(8,128)S(1)}, f32[3,4,16,1]{3,2,1,0:T(8,128)S(1)}, u32[]{:S(2)}, u32[]{:S(2)}) %collective-permute-start.17) | collective-permute-done | bytes 800 | tf_op jit(solution)/shard_map/ppermute | solution.py:16
  304.6 151.5 %all-reduce.1 = (f32[]{:T(128)}, f32[]{:T(128)}) all-reduce(f32[]{:T(128)} %get-tuple-element.3, f32[]{:T(128)} %get-tuple-element.2), channel_id=1, replica_groups=mesh['dia'=8,'sub'=32,'rad'=4] {'dia','sub','rad'}, use_global_device_ids=true, to_apply=%region_6.7 | all-reduce | flops 2 | bytes 16 | tf_op jit(solution)/shard_map/psum | solution.py:33
  464.6 3.8 collective-permute-done.18
  468.5 3.8 collective-permute-start.20
  472.3 10.5 %collective-permute-start.21 = (f32[3,6,1,1024]{3,2,1,0:T(1,128)S(1)}, f32[3,6,1,1024]{3,2,1,0:T(1,128)S(1)}, u32[]{:S(2)}, u32[]{:S(2)}) collective-permute-start(f32[3,6,1,1024]{3,2,1,0:T(1,128)S(1)} %get-tuple-element.27), channel_id=1, source_target_pairs={{0,4},{4,8},{8,12},{12,16},{16,20},{20,24},{24,28},{28,32},{32,36}... | collective-permute-start | bytes 221192 | tf_op jit(solution)/shard_map/ppermute | solution.py:16
  482.9 5.1 collective-permute-start.22
  490.3 9.6 %collective-permute-done.23 = f32[3,4,16,1]{3,2,1,0:T(8,128)S(1)} collective-permute-done((f32[3,4,16,1]{3,2,1,0:T(8,128)S(1)}, f32[3,4,16,1]{3,2,1,0:T(8,128)S(1)}, u32[]{:S(2)}, u32[]{:S(2)}) %collective-permute-start.23) | collective-permute-done | bytes 800 | tf_op jit(solution)/shard_map/ppermute | solution.py:16
  501.2 151.5 %all-reduce = (f32[]{:T(128)}, f32[]{:T(128)}) all-reduce(f32[]{:T(128)} %get-tuple-element.12, f32[]{:T(128)} %fusion.3), channel_id=1, replica_groups=mesh['dia'=8,'sub'=32,'rad'=4] {'dia','sub','rad'}, use_global_device_ids=true, to_apply=%region_10.11 | all-reduce | flops 2 | bytes 16 | tf_op jit(solution)/shard_map/psum | solution.py:33
  (87 shorter events, 39.6 us)
Async XLA Ops:
  3.0 20.2 %collective-permute-start.1 = (f32[5,1,16,1024]{3,2,1,0:T(8,128)S(1)}, f32[5,1,16,1024]{3,2,1,0:T(8,128)S(1)}, u32[]{:S(2)}, u32[]{:S(2)}) collective-permute-start(f32[5,1,16,1024]{3,2,1,0:T(8,128)S(1)} %get-tuple-element.22), channel_id=1, source_target_pairs={{0,1},{1,2},{2,3},{4,5},{5,6},{6,7},{8,9},{9,10},{10,11},{12,13},{... | collective-permute-start | bytes 983048 | tf_op jit(solution)/shard_map/ppermute | solution.py:16
  7.0 16.3 %collective-permute-start = (f32[5,1,16,1024]{3,2,1,0:T(8,128)S(1)}, f32[5,1,16,1024]{3,2,1,0:T(8,128)S(1)}, u32[]{:S(2)}, u32[]{:S(2)}) collective-permute-start(f32[5,1,16,1024]{3,2,1,0:T(8,128)S(1)} %get-tuple-element.23), channel_id=1, source_target_pairs={{1,0},{2,1},{3,2},{5,4},{6,5},{7,6},{9,8},{10,9},{11,10},{13,12},{... | collective-permute-start | bytes 983048 | tf_op jit(solution)/shard_map/ppermute | solution.py:19
  8.4 33.6 %collective-permute-start.4 = (f32[5,4,16,1]{3,2,1,0:T(8,128)S(1)}, f32[5,4,16,1]{3,2,1,0:T(8,128)S(1)}, u32[]{:S(2)}, u32[]{:S(2)}) collective-permute-start(f32[5,4,16,1]{3,2,1,0:T(8,128)S(1)} %get-tuple-element.24), channel_id=1, source_target_pairs={{128,0},{256,128},{384,256},{512,384},{640,512},{768,640},{896,768... | collective-permute-start | bytes 3848 | tf_op jit(solution)/shard_map/ppermute | solution.py:19
  21.3 20.7 %collective-permute-start.5 = (f32[5,4,16,1]{3,2,1,0:T(8,128)S(1)}, f32[5,4,16,1]{3,2,1,0:T(8,128)S(1)}, u32[]{:S(2)}, u32[]{:S(2)}) collective-permute-start(f32[5,4,16,1]{3,2,1,0:T(8,128)S(1)} %get-tuple-element.25), channel_id=1, source_target_pairs={{0,128},{128,256},{256,384},{384,512},{512,640},{640,768},{768,896... | collective-permute-start | bytes 3848 | tf_op jit(solution)/shard_map/ppermute | solution.py:16
  23.5 22.2 %collective-permute-start.2 = (f32[5,6,1,1024]{3,2,1,0:T(1,128)S(1)}, f32[5,6,1,1024]{3,2,1,0:T(1,128)S(1)}, u32[]{:S(2)}, u32[]{:S(2)}) collective-permute-start(f32[5,6,1,1024]{3,2,1,0:T(1,128)S(1)} %get-tuple-element.18), channel_id=1, source_target_pairs={{4,0},{8,4},{12,8},{16,12},{20,16},{24,20},{28,24},{32,28},{36,32}... | collective-permute-start | bytes 368648 | tf_op jit(solution)/shard_map/ppermute | solution.py:19
  29.6 16.1 %collective-permute-start.3 = (f32[5,6,1,1024]{3,2,1,0:T(1,128)S(1)}, f32[5,6,1,1024]{3,2,1,0:T(1,128)S(1)}, u32[]{:S(2)}, u32[]{:S(2)}) collective-permute-start(f32[5,6,1,1024]{3,2,1,0:T(1,128)S(1)} %get-tuple-element.19), channel_id=1, source_target_pairs={{0,4},{4,8},{8,12},{12,16},{16,20},{20,24},{24,28},{28,32},{32,36}... | collective-permute-start | bytes 368648 | tf_op jit(solution)/shard_map/ppermute | solution.py:16
  46.5 7.7 %collective-permute-start.7 = (f32[3,1,16,1024]{3,2,1,0:T(8,128)S(1)}, f32[3,1,16,1024]{3,2,1,0:T(8,128)S(1)}, u32[]{:S(2)}, u32[]{:S(2)}) collective-permute-start(f32[3,1,16,1024]{3,2,1,0:T(8,128)S(1)} %get-tuple-element.40), channel_id=1, source_target_pairs={{0,1},{1,2},{2,3},{4,5},{5,6},{6,7},{8,9},{9,10},{10,11},{12,13},{... | collective-permute-start | bytes 589832 | tf_op jit(solution)/shard_map/ppermute | solution.py:16
  51.6 6.4 collective-permute-start.6
  58.1 39.3 %collective-permute-start.8 = (f32[3,6,1,1024]{3,2,1,0:T(1,128)S(1)}, f32[3,6,1,1024]{3,2,1,0:T(1,128)S(1)}, u32[]{:S(2)}, u32[]{:S(2)}) collective-permute-start(f32[3,6,1,1024]{3,2,1,0:T(1,128)S(1)} %get-tuple-element.30), channel_id=1, source_target_pairs={{4,0},{8,4},{12,8},{16,12},{20,16},{24,20},{28,24},{32,28},{36,32}... | collective-permute-start | bytes 221192 | tf_op jit(solution)/shard_map/ppermute | solution.py:19
  60.1 37.4 %collective-permute-start.9 = (f32[3,6,1,1024]{3,2,1,0:T(1,128)S(1)}, f32[3,6,1,1024]{3,2,1,0:T(1,128)S(1)}, u32[]{:S(2)}, u32[]{:S(2)}) collective-permute-start(f32[3,6,1,1024]{3,2,1,0:T(1,128)S(1)} %get-tuple-element.31), channel_id=1, source_target_pairs={{0,4},{4,8},{8,12},{12,16},{16,20},{20,24},{24,28},{28,32},{32,36}... | collective-permute-start | bytes 221192 | tf_op jit(solution)/shard_map/ppermute | solution.py:16
  72.5 15.6 %collective-permute-start.10 = (f32[3,4,16,1]{3,2,1,0:T(8,128)S(1)}, f32[3,4,16,1]{3,2,1,0:T(8,128)S(1)}, u32[]{:S(2)}, u32[]{:S(2)}) collective-permute-start(f32[3,4,16,1]{3,2,1,0:T(8,128)S(1)} %get-tuple-element.42), channel_id=1, source_target_pairs={{128,0},{256,128},{384,256},{512,384},{640,512},{768,640},{896,768... | collective-permute-start | bytes 2312 | tf_op jit(solution)/shard_map/ppermute | solution.py:19
  85.5 12.0 %collective-permute-start.11 = (f32[3,4,16,1]{3,2,1,0:T(8,128)S(1)}, f32[3,4,16,1]{3,2,1,0:T(8,128)S(1)}, u32[]{:S(2)}, u32[]{:S(2)}) collective-permute-start(f32[3,4,16,1]{3,2,1,0:T(8,128)S(1)} %get-tuple-element.43), channel_id=1, source_target_pairs={{0,128},{128,256},{256,384},{384,512},{512,640},{640,768},{768,896... | collective-permute-start | bytes 2312 | tf_op jit(solution)/shard_map/ppermute | solution.py:16
  256.4 6.3 collective-permute-start.13
  259.1 7.3 %collective-permute-start.12 = (f32[3,1,16,1024]{3,2,1,0:T(8,128)S(1)}, f32[3,1,16,1024]{3,2,1,0:T(8,128)S(1)}, u32[]{:S(2)}, u32[]{:S(2)}) collective-permute-start(f32[3,1,16,1024]{3,2,1,0:T(8,128)S(1)} %get-tuple-element.37), channel_id=1, source_target_pairs={{1,0},{2,1},{3,2},{5,4},{6,5},{7,6},{9,8},{10,9},{11,10},{13,12},{... | collective-permute-start | bytes 589832 | tf_op jit(solution)/shard_map/ppermute | solution.py:19
  266.6 35.8 %collective-permute-start.14 = (f32[3,6,1,1024]{3,2,1,0:T(1,128)S(1)}, f32[3,6,1,1024]{3,2,1,0:T(1,128)S(1)}, u32[]{:S(2)}, u32[]{:S(2)}) collective-permute-start(f32[3,6,1,1024]{3,2,1,0:T(1,128)S(1)} %get-tuple-element.28), channel_id=1, source_target_pairs={{4,0},{8,4},{12,8},{16,12},{20,16},{24,20},{28,24},{32,28},{36,32}... | collective-permute-start | bytes 221192 | tf_op jit(solution)/shard_map/ppermute | solution.py:19
  270.4 32.0 %collective-permute-start.15 = (f32[3,6,1,1024]{3,2,1,0:T(1,128)S(1)}, f32[3,6,1,1024]{3,2,1,0:T(1,128)S(1)}, u32[]{:S(2)}, u32[]{:S(2)}) collective-permute-start(f32[3,6,1,1024]{3,2,1,0:T(1,128)S(1)} %get-tuple-element.29), channel_id=1, source_target_pairs={{0,4},{4,8},{8,12},{12,16},{16,20},{20,24},{24,28},{28,32},{32,36}... | collective-permute-start | bytes 221192 | tf_op jit(solution)/shard_map/ppermute | solution.py:16
  281.0 11.4 %collective-permute-start.16 = (f32[3,4,16,1]{3,2,1,0:T(8,128)S(1)}, f32[3,4,16,1]{3,2,1,0:T(8,128)S(1)}, u32[]{:S(2)}, u32[]{:S(2)}) collective-permute-start(f32[3,4,16,1]{3,2,1,0:T(8,128)S(1)} %get-tuple-element.38), channel_id=1, source_target_pairs={{128,0},{256,128},{384,256},{512,384},{640,512},{768,640},{896,768... | collective-permute-start | bytes 2312 | tf_op jit(solution)/shard_map/ppermute | solution.py:19
  290.4 12.0 %collective-permute-start.17 = (f32[3,4,16,1]{3,2,1,0:T(8,128)S(1)}, f32[3,4,16,1]{3,2,1,0:T(8,128)S(1)}, u32[]{:S(2)}, u32[]{:S(2)}) collective-permute-start(f32[3,4,16,1]{3,2,1,0:T(8,128)S(1)} %get-tuple-element.39), channel_id=1, source_target_pairs={{0,128},{128,256},{256,384},{384,512},{512,640},{640,768},{768,896... | collective-permute-start | bytes 2312 | tf_op jit(solution)/shard_map/ppermute | solution.py:16
  459.4 5.1 collective-permute-start.19
  461.1 7.3 %collective-permute-start.18 = (f32[3,1,16,1024]{3,2,1,0:T(8,128)S(1)}, f32[3,1,16,1024]{3,2,1,0:T(8,128)S(1)}, u32[]{:S(2)}, u32[]{:S(2)}) collective-permute-start(f32[3,1,16,1024]{3,2,1,0:T(8,128)S(1)} %get-tuple-element.33), channel_id=1, source_target_pairs={{1,0},{2,1},{3,2},{5,4},{6,5},{7,6},{9,8},{10,9},{11,10},{13,12},{... | collective-permute-start | bytes 589832 | tf_op jit(solution)/shard_map/ppermute | solution.py:19
  468.5 31.5 %collective-permute-start.20 = (f32[3,6,1,1024]{3,2,1,0:T(1,128)S(1)}, f32[3,6,1,1024]{3,2,1,0:T(1,128)S(1)}, u32[]{:S(2)}, u32[]{:S(2)}) collective-permute-start(f32[3,6,1,1024]{3,2,1,0:T(1,128)S(1)} %get-tuple-element.26), channel_id=1, source_target_pairs={{4,0},{8,4},{12,8},{16,12},{20,16},{24,20},{28,24},{32,28},{36,32}... | collective-permute-start | bytes 221192 | tf_op jit(solution)/shard_map/ppermute | solution.py:19
  472.3 27.7 %collective-permute-start.21 = (f32[3,6,1,1024]{3,2,1,0:T(1,128)S(1)}, f32[3,6,1,1024]{3,2,1,0:T(1,128)S(1)}, u32[]{:S(2)}, u32[]{:S(2)}) collective-permute-start(f32[3,6,1,1024]{3,2,1,0:T(1,128)S(1)} %get-tuple-element.27), channel_id=1, source_target_pairs={{0,4},{4,8},{8,12},{12,16},{16,20},{20,24},{24,28},{28,32},{32,36}... | collective-permute-start | bytes 221192 | tf_op jit(solution)/shard_map/ppermute | solution.py:16
  482.9 7.5 %collective-permute-start.22 = (f32[3,4,16,1]{3,2,1,0:T(8,128)S(1)}, f32[3,4,16,1]{3,2,1,0:T(8,128)S(1)}, u32[]{:S(2)}, u32[]{:S(2)}) collective-permute-start(f32[3,4,16,1]{3,2,1,0:T(8,128)S(1)} %get-tuple-element.34), channel_id=1, source_target_pairs={{128,0},{256,128},{384,256},{512,384},{640,512},{768,640},{896,768... | collective-permute-start | bytes 2312 | tf_op jit(solution)/shard_map/ppermute | solution.py:19
  488.0 12.0 %collective-permute-start.23 = (f32[3,4,16,1]{3,2,1,0:T(8,128)S(1)}, f32[3,4,16,1]{3,2,1,0:T(8,128)S(1)}, u32[]{:S(2)}, u32[]{:S(2)}) collective-permute-start(f32[3,4,16,1]{3,2,1,0:T(8,128)S(1)} %get-tuple-element.35), channel_id=1, source_target_pairs={{0,128},{128,256},{256,384},{384,512},{512,640},{640,768},{768,896... | collective-permute-start | bytes 2312 | tf_op jit(solution)/shard_map/ppermute | solution.py:16
  (16 other events, 500.7 us)
where the time goes:
time: 658 us; the launch traced here: 657 us
  blocking collectives  457 us (69%)
  starting transfers between devices  128 us (19%)
  waiting for transfers between devices  50.3 us (8%)
  other arithmetic  14.8 us (2%)
    psum x3, blocking collectives, inner_sums(): return lax.psum((first, second), ('dia', 'sub', 'rad'))  457 us
    ppermute x12, starting transfers between devices, padded(): lax.ppermute(lax.slice_in_dim(block, block.shape[dim] - width, None, axis...  66.8 us
    ppermute x12, starting transfers between devices, padded(): lax.ppermute(lax.slice_in_dim(block, 0, width, axis=dim), axis, backward)  61.1 us
    ppermute x12, waiting for transfers between devices, padded(): lax.ppermute(lax.slice_in_dim(block, block.shape[dim] - width, None, axis...  34.7 us
    ppermute x12, waiting for transfers between devices, padded(): lax.ppermute(lax.slice_in_dim(block, 0, width, axis=dim), axis, backward)  15.5 us
  transfers between devices with their start and end apart: 24, of which 12 were waited for; matrix products, arithmetic and copies ran while one was open for 0% of the time, Pallas kernels for 0%

commit v1 on v0

v1 whole, which is shorter than its diff:
```python
import functools

import jax
import jax.numpy as jnp
from jax import lax
from jax.experimental import pallas as pl
from jax.experimental.pallas import tpu as pltpu
from jax.sharding import PartitionSpec as P

MESH = pl.DeviceIdType.MESH
H = 4
Y_COUNT, CORES = 4, 2
ALPHA_LOW, ALPHA_HIGH = 0.5, 62.0


def later(x, axis):
    return pltpu.roll(x, x.shape[axis] - 1, axis)


def earlier(x, axis):
    return pltpu.roll(x, 1, axis)


def places(sizes):
    n_dia, n_sub, n_rad, n_y, n_core = sizes
    n_zh = n_sub // (n_y * n_core)
    dia, sub, rad = lax.axis_index("dia"), lax.axis_index("sub"), lax.axis_index("rad")
    y, zh, core = sub // (n_zh * n_core), (sub // n_core) % n_zh, sub % n_core
    n_z = n_zh * n_dia
    n_g = n_rad * n_y * n_core
    z = zh * n_dia + dia
    g = (rad * n_y + y) * n_core + core

    def along_z(k):
        t = lax.rem(z + k, n_z)
        return {"sub": (y * n_zh + t // n_dia) * n_core + core, "dia": t % n_dia}

    def in_plane(k):
        t = lax.rem(g + k, n_g)
        r2, y2, c2 = t // (n_y * n_core), (t // n_core) % n_y, t % n_core
        return {"sub": (y2 * n_zh + zh) * n_core + c2, "rad": r2}

    return dia, sub, rad, core, z, g, n_z, n_g, along_z, in_plane


def kernel(
    sizes, table, s_hbm, t_hbm, f_hbm, m_hbm, temp_hbm, vel_hbm,
    s_v, d_v, m_v, T, Q, I, z0, z1, z2, eu0, ed0,
    sub_out, sub_in, dia_out, dia_in, mine, plane, column, temp_v, vel_v,
    load_sem, store_sem, dia_s, dia_r, rad_s, rad_r, sub_s, sub_r, cor_s, cor_r, fwd_s, fwd_r,
    plane_s, plane_r, column_s, column_r, relay,
):
    n_dia, n_sub, n_rad, n_y, n_core = sizes
    layers, rows, width = s_v.shape
    full_rows, full = rows + 8, width + 128
    dia, sub, rad, core, z, g, n_z, n_g, along_z, in_plane = places(sizes)
    reach = max(1, n_z // 4)
    own = pl.ds(H, layers)
    near = [k for k in range(1, n_z) if min(k, n_z - k) <= reach]

    has_up, has_down = sub < n_sub - 1, sub > 0
    has_above, has_below = rad < n_rad - 1, rad > 0
    above, below = {"rad": jnp.minimum(rad + 1, n_rad - 1)}, {"rad": jnp.maximum(rad - 1, 0)}
    up, down = {"sub": jnp.minimum(sub + 1, n_sub - 1)}, {"sub": jnp.maximum(sub - 1, 0)}
    right, left = {"dia": lax.rem(dia + 1, n_dia)}, {"dia": lax.rem(dia + n_dia - 1, n_dia)}

    barrier = pltpu.get_barrier_semaphore()
    for k in near:
        pl.semaphore_signal(barrier, inc=1, device_id=along_z(k), device_id_type=MESH)
    far_up = jnp.logical_and(core == n_core - 1, has_up)
    far_down = jnp.logical_and(core == 0, has_down)

    @pl.when(far_up)
    def _():
        pl.semaphore_signal(barrier, inc=1, device_id=up, device_id_type=MESH)

    @pl.when(far_down)
    def _():
        pl.semaphore_signal(barrier, inc=1, device_id=down, device_id_type=MESH)

    for k in range(1, n_g):
        pl.semaphore_signal(barrier, inc=1, device_id=in_plane(k), device_id_type=MESH)

    loads = [
        pltpu.make_async_copy(s_hbm, s_v, load_sem.at[0]),
        pltpu.make_async_copy(f_hbm, d_v, load_sem.at[1]),
        pltpu.make_async_copy(t_hbm, T.at[own, pl.ds(0, rows), pl.ds(0, width)], load_sem.at[2]),
        pltpu.make_async_copy(m_hbm, m_v, load_sem.at[3]),
    ]
    for copy in loads:
        copy.start()
    for copy in loads:
        copy.wait()

    lane = lax.broadcasted_iota(jnp.int32, (1, width), 1)
    picks = [table[i] for i in range(2)]
    choice = jnp.where(lane < width // 2, picks[0], picks[1])

    def motion(c, layer, row=slice(None)):
        return jnp.where(
            choice == 0,
            m_v[0, c, layer].astype(jnp.float32)[row],
            m_v[1, c, layer].astype(jnp.float32)[row],
        )

    def prepare(layer, carry):
        s = s_v[layer]
        diagonal = 6.0 + d_v[layer]
        d_v[layer] = diagonal
        inverse = 1.0 / diagonal
        I[H + layer, :rows, :width] = inverse
        Q[H + layer, :rows, :width] = -0.5 * s * inverse
        v = motion(0, layer)
        eu0[layer + 1] = (0.25 + 0.125 * v) * s
        ed0[layer + 1] = (0.25 - 0.125 * v) * s
        return carry

    lax.fori_loop(0, layers, prepare, 0)

    def pack(columns, edge):
        for l in range(layers):
            sub_out[0, l, 0:4, columns] = T[H + l, rows - 4 : rows, columns]
            sub_out[0, l, 4:7, columns] = Q[H + l, rows - 3 : rows, columns]
            sub_out[0, layers, 2 * l : 2 * l + 2, columns] = I[H + l, rows - 2 : rows, columns]
            sub_out[1, l, 0:4, columns] = T[H + l, 0:4, columns]
            sub_out[1, l, 4:7, columns] = Q[H + l, 0:3, columns]
            sub_out[1, layers, 2 * l : 2 * l + 2, columns] = I[H + l, 0:2, columns]
            if edge:
                v = motion(1, l)
                s = s_v[l]
                sub_out[0, l, 7:8, columns] = ((0.25 - 0.125 * v) * s)[rows - 1 : rows]
                sub_out[1, l, 7:8, columns] = ((0.25 + 0.125 * v) * s)[0:1]
            else:
                sub_out[0, l, 7:8, columns] = T[H + l, 0:1, columns]
                sub_out[1, l, 7:8, columns] = T[H + l, 0:1, columns]

    main, side = slice(0, width), slice(width, full)
    pack(main, True)

    tile_lane = lax.broadcasted_iota(jnp.int32, (1, 128), 1)
    packed = [jnp.zeros((8, 128), jnp.float32), jnp.zeros((8, 128), jnp.float32)]
    for l in range(layers):
        for half in range(rows // 8):
            k = l * (rows // 8) + half
            group = slice(8 * half, 8 * half + 8)
            for side_at, at in ((0, slice(width - 128, width)), (1, slice(0, 128))):
                pick = picks[1] if side_at == 0 else picks[0]
                v = jnp.where(
                    pick == 0,
                    m_v[0, 2, l, :, at].astype(jnp.float32)[group],
                    m_v[1, 2, l, :, at].astype(jnp.float32)[group],
                )
                sign = -0.125 if side_at == 0 else 0.125
                e = (0.25 + sign * v) * s_v[l, group, at]
                items = (T[H + l, group, at], Q[H + l, group, at], I[H + l, group, at], e)
                tile = packed[side_at]
                for n, item in enumerate(items):
                    if side_at == 0:
                        low = 124 - 4 * n - 16 * k
                        moved = pltpu.roll(item, (low - 124) % 128, 1)
                    else:
                        low = 4 * n + 16 * k
                        moved = pltpu.roll(item, low % 128, 1)
                    tile = jnp.where((tile_lane >= low) & (tile_lane < low + 4), moved, tile)
                packed[side_at] = tile
    dia_out[0] = packed[0]
    dia_out[1] = packed[1]

    halo_low, halo_high = pl.ds(0, H), pl.ds(H + layers, H)

    @pl.when(jnp.logical_not(has_below))
    def _():
        for ref in (T, Q, I):
            ref[halo_low] = jnp.zeros((H, full_rows, full), jnp.float32)
        ed0[0] = jnp.zeros((rows, width), jnp.float32)

    @pl.when(jnp.logical_not(has_above))
    def _():
        for ref in (T, Q, I):
            ref[halo_high] = jnp.zeros((H, full_rows, full), jnp.float32)
        eu0[layers + 1] = jnp.zeros((rows, width), jnp.float32)

    @pl.when(jnp.logical_not(has_down))
    def _():
        sub_in[0] = jnp.zeros(sub_in.shape[1:], jnp.float32)

    @pl.when(jnp.logical_not(has_up))
    def _():
        sub_in[1] = jnp.zeros(sub_in.shape[1:], jnp.float32)

    pl.semaphore_wait(
        barrier, len(near) + n_g - 1 + far_up.astype(jnp.int32) + far_down.astype(jnp.int32)
    )

    def send(src, dst, ssem, rsem, device):
        return pltpu.make_async_remote_copy(
            src_ref=src, dst_ref=dst, send_sem=ssem, recv_sem=rsem,
            device_id=device, device_id_type=MESH,
        )

    here, there = slice(0, width), slice(width, full)
    sub_main = [
        send(sub_out.at[i, :, :, pl.ds(0, width)], sub_in.at[i, :, :, pl.ds(0, width)], sub_s.at[i], sub_r.at[i], to)
        for i, to in enumerate((up, down))
    ]
    sub_side = [
        send(sub_out.at[i, :, :, pl.ds(width, 128)], sub_in.at[i, :, :, pl.ds(width, 128)], cor_s.at[i], cor_r.at[i], to)
        for i, to in enumerate((up, down))
    ]
    dia_copies = [
        send(dia_out.at[i], dia_in.at[i], dia_s.at[i], dia_r.at[i], to)
        for i, to in enumerate((right, left))
    ]

    def slab(ref, first, count, rows_at, lanes_at):
        return ref.at[pl.ds(first, count), pl.ds(*rows_at), pl.ds(*lanes_at)]

    def layer_copies(counts, rows_at, lanes_at, ssem, rsem):
        both = [[], []]
        for n, (ref, count) in enumerate(zip((T, Q, I), counts)):
            both[0].append(send(
                slab(ref, H + layers - count, count, rows_at, lanes_at),
                slab(ref, H - count, count, rows_at, lanes_at),
                ssem.at[0, n], rsem.at[0, n], above,
            ))
            both[1].append(send(
                slab(ref, H, count, rows_at, lanes_at),
                slab(ref, H + layers, count, rows_at, lanes_at),
                ssem.at[1, n], rsem.at[1, n], below,
            ))
        return both

    rad_main = layer_copies((4, 3, 2), (0, rows), (0, width), rad_s, rad_r)
    rad_main[0].append(send(ed0.at[layers], ed0.at[0], rad_s.at[0, 3], rad_r.at[0, 3], above))
    rad_main[1].append(send(eu0.at[1], eu0.at[layers + 1], rad_s.at[1, 3], rad_r.at[1, 3], below))
    rad_side = layer_copies((3, 2, 1), (0, rows), (width, 128), fwd_s.at[0], fwd_r.at[0])
    rad_rows = layer_copies((3, 2, 1), (rows, 8), (0, full), fwd_s.at[1], fwd_r.at[1])

    def start(copies, flag):
        @pl.when(flag)
        def _():
            for copy in copies:
                copy.start()

    def arrived(copies, flag):
        @pl.when(flag)
        def _():
            for copy in copies:
                copy.wait_recv()

    def left_here(copies, flag):
        @pl.when(flag)
        def _():
            for copy in copies:
                copy.wait_send()

    start([sub_main[0]], has_up)
    start([sub_main[1]], has_down)
    for copy in dia_copies:
        copy.start()
    start(rad_main[0], has_above)
    start(rad_main[1], has_below)

    for k in sorted({reach, n_z - reach}):
        pl.semaphore_signal(relay, inc=1, device_id=along_z(k), device_id_type=MESH)

    for copy in dia_copies:
        copy.wait_recv()
    eu2_side, ed2_side = [], []
    for l in range(layers):
        for half in range(rows // 8):
            k = l * (rows // 8) + half
            group = slice(8 * half, 8 * half + 8)
            for n, ref in enumerate((T, Q, I)):
                from_left = pltpu.roll(dia_in[0], (4 * n + 16 * k) % 128, 1)
                from_right = pltpu.roll(dia_in[1], (-4 * n - 16 * k) % 128, 1)
                ref[H + l, group, width:full] = jnp.where(tile_lane < 64, from_right, from_left)
    pack(side, False)
    start([sub_side[0]], has_up)
    start([sub_side[1]], has_down)
    start(rad_side[0], has_above)
    start(rad_side[1], has_below)

    def unpack(columns):
        for l in range(layers):
            T[H + l, rows + 4 : rows + 8, columns] = sub_in[0, l, 0:4, columns]
            Q[H + l, rows + 5 : rows + 8, columns] = sub_in[0, l, 4:7, columns]
            I[H + l, rows + 6 : rows + 8, columns] = sub_in[0, layers, 2 * l : 2 * l + 2, columns]
            T[H + l, rows : rows + 4, columns] = sub_in[1, l, 0:4, columns]
            Q[H + l, rows : rows + 3, columns] = sub_in[1, l, 4:7, columns]
            I[H + l, rows : rows + 2, columns] = sub_in[1, layers, 2 * l : 2 * l + 2, columns]

    arrived([sub_main[0]], has_down)
    arrived([sub_main[1]], has_up)
    unpack(main)
    arrived([sub_side[0]], has_down)
    arrived([sub_side[1]], has_up)
    unpack(side)
    start(rad_rows[0], has_above)
    start(rad_rows[1], has_below)
    for group in (rad_main, rad_side, rad_rows):
        arrived(group[0], has_below)
        arrived(group[1], has_above)

    def first(L, carry):
        t, q = T[L], Q[L]
        z0[0, L] = q * (T[L + 1] - T[L - 1])
        z0[1, L] = q * (later(t, 0) - earlier(t, 0))
        z0[2, L] = q * (later(t, 1) - earlier(t, 1))
        return carry

    lax.fori_loop(1, layers + 2 * H - 1, first, 0)

    def beside(ref, c, L):
        x = ref[c, L]
        rows_sum = later(x, 0) + earlier(x, 0)
        lanes_sum = later(x, 1) + earlier(x, 1)
        return ref[c, L + 1] + ref[c, L - 1] + rows_sum + lanes_sum

    def second(L, carry):
        for c in range(3):
            z1[c, L] = I[L] * beside(z0, c, L)
        return carry

    lax.fori_loop(2, layers + 2 * H - 2, second, 0)

    def third(L, carry):
        for c in range(3):
            z2[c, L] = I[L] * beside(z1, c, L)
        return carry

    lax.fori_loop(3, layers + 2 * H - 3, third, 0)

    def folded(x):
        total = jnp.zeros((8, 128), jnp.float32)
        for r in range(0, rows, 8):
            for w in range(0, width, 128):
                total = total + x[r : r + 8, w : w + 128]
        return total

    def moments(l, sums):
        L = H + l
        d = d_v[l]
        new = [0.0] * 6
        for c in range(3):
            a, b, e = z0[c, L, :rows, :width], z1[c, L, :rows, :width], z2[c, L, :rows, :width]
            y = beside(z2, c, L)[:rows, :width]
            da, db, de = d * a, d * b, d * e
            for j, term in enumerate((da * a, da * b, db * b, db * e, de * e, e * y)):
                new[j] = new[j] + term
        return tuple(total + folded(x) for total, x in zip(sums, new))

    sums = lax.fori_loop(0, layers, moments, (jnp.zeros((8, 128), jnp.float32),) * 6)

    row = jnp.zeros((1, 128), jnp.float32)
    for j in range(6):
        row = jnp.where(tile_lane == j, jnp.sum(sums[j], keepdims=True), row)

    def exchange(value, slots, count, index, peer, ssem, rsem, order):
        mine[...] = value
        slots[index] = value
        for k in order:
            send(mine, slots.at[index], ssem, rsem, peer(k)).start()
        return send(slots.at[pl.ds(0, count - 1)], slots.at[pl.ds(0, count - 1)], ssem, rsem, peer(1))

    copies = exchange(row, plane, n_g, g, in_plane, plane_s, plane_r, range(1, n_g))
    copies.wait_recv()
    copies.wait_send()
    row = jnp.sum(plane[...], axis=0)
    far_first = sorted(range(1, n_z), key=lambda k: -min(k, n_z - k))
    pl.semaphore_wait(relay, len({reach, n_z - reach}))
    copies = exchange(row, column, n_z, z, along_z, column_s, column_r, far_first)

    def advect(l, carry):
        s = s_v[l]
        v1, v2 = motion(1, l), motion(2, l)
        row_at = lax.broadcasted_iota(jnp.int32, (rows, width), 0)
        total = -0.5 * s + eu0[l + 2] + ed0[l]
        u, w = (0.25 + 0.125 * v1) * s, (0.25 - 0.125 * v1) * s
        total = total + jnp.where(row_at == rows - 1, sub_in[1, l, 7:8, :width], later(u, 0))
        total = total + jnp.where(row_at == 0, sub_in[0, l, 7:8, :width], earlier(w, 0))
        u, w = (0.25 + 0.125 * v2) * s, (0.25 - 0.125 * v2) * s
        temp_v[l] = total + later(u, 1) + earlier(w, 1)
        return carry

    lax.fori_loop(0, layers, advect, 0)
    for l in range(layers):
        for half in range(rows // 8):
            k = l * (rows // 8) + half
            group = slice(8 * half, 8 * half + 8)
            s_low, s_high = s_v[l, group, 0:128], s_v[l, group, width - 128 : width]

            def speed(at, pick, group=group, l=l):
                return jnp.where(
                    pick == 0,
                    m_v[0, 2, l, :, at].astype(jnp.float32)[group],
                    m_v[1, 2, l, :, at].astype(jnp.float32)[group],
                )

            low, high = slice(0, 128), slice(width - 128, width)
            u = pltpu.roll((0.25 + 0.125 * speed(low, picks[0])) * s_low, 127, 1)
            w = pltpu.roll((0.25 - 0.125 * speed(high, picks[1])) * s_high, 1, 1)
            from_left = pltpu.roll(dia_in[0], (13 + 16 * k) % 128, 1)
            from_right = pltpu.roll(dia_in[1], (127 - 12 - 16 * k) % 128, 1)
            temp_v[l, group, low] += jnp.where(tile_lane == 0, from_left - w, 0.0)
            temp_v[l, group, high] += jnp.where(tile_lane == 127, from_right - u, 0.0)

    copies.wait_recv()
    copies.wait_send()
    row = jnp.sum(column[...], axis=0)
    m0, m1, m2, m3, m4, m5 = (
        jnp.sum(jnp.where(tile_lane == j, row, 0.0), axis=1, keepdims=True) for j in range(6)
    )

    def step(p):
        a, b, c = p
        square = (a * a, 2.0 * a * b, b * b + 2.0 * a * c, 2.0 * b * c, c * c)
        energy = sum(x * m for x, m in zip(square, (m0, m1, m2, m3, m4)))
        moved = sum(x * m for x, m in zip(square, (m1, m2, m3, m4, m5)))
        return jnp.clip(energy / (energy - moved), ALPHA_LOW, ALPHA_HIGH)

    one, none = jnp.ones_like(m0), jnp.zeros_like(m0)
    p0 = (one, none, none)
    alpha0 = step(p0)
    p1 = (1.0 - alpha0, alpha0, none)
    alpha1 = step(p1)
    p2 = (p1[0] * (1.0 - alpha1), p1[1] * (1.0 - alpha1) + p1[0] * alpha1, p1[1] * alpha1)
    alpha2 = step(p2)
    c0, c1, c2 = (alpha0 * x + alpha1 * y + alpha2 * w for x, y, w in zip(p0, p1, p2))

    stores = []
    for l in range(layers):
        stores.append(pltpu.make_async_copy(vel_v.at[:, l], vel_hbm.at[:, l], store_sem.at[0, l]))
        stores.append(pltpu.make_async_copy(temp_v.at[l], temp_hbm.at[l], store_sem.at[1, l]))
        for c in range(3):
            at = (c, H + l, slice(0, rows), slice(0, width))
            velocity = c0 * z0[at] + c1 * z1[at] + c2 * z2[at]
            vel_v[c, l] = velocity
            if c == 0:
                temp_v[l] = temp_v[l] + 4.0 * velocity
        stores[-2].start()
        stores[-1].start()

    left_here([sub_main[0], sub_side[0]], has_up)
    left_here([sub_main[1], sub_side[1]], has_down)
    for copy in dia_copies:
        copy.wait_send()
    for group in (rad_main, rad_side, rad_rows):
        left_here(group[0], has_above)
        left_here(group[1], has_below)
    for copy in stores:
        copy.wait()


def solution(mesh):
    shape = mesh.shape
    n_y = Y_COUNT if shape["sub"] >= 32 else 1
    sizes = (shape["dia"], shape["sub"], shape["rad"], n_y, CORES)
    n_z = shape["dia"] * shape["sub"] // (n_y * CORES)
    n_g = shape["rad"] * n_y * CORES

    def shards(sensitivity_heat, stored_heat, friction_diagonal, stored_motions, record_choice_table):
        layers, rows, width = sensitivity_heat.shape
        tall, wide, long = layers + 2 * H, rows + 8, width + 128
        f32 = jnp.float32
        block = pltpu.VMEM((layers, rows, width), f32)
        field = pltpu.VMEM((tall, wide, long), f32)
        vector = pltpu.VMEM((3, tall, wide, long), f32)
        dma = pltpu.SemaphoreType.DMA
        anywhere = pl.BlockSpec(memory_space=pl.ANY)
        return pl.pallas_call(
            functools.partial(kernel, sizes),
            out_shape=(
                jax.ShapeDtypeStruct((layers, rows, width), f32),
                jax.ShapeDtypeStruct((3, layers, rows, width), f32),
            ),
            in_specs=[pl.BlockSpec(memory_space=pltpu.SMEM)] + [anywhere] * 4,
            out_specs=(anywhere, anywhere),
            scratch_shapes=[
                block, block, pltpu.VMEM(stored_motions.shape, stored_motions.dtype),
                field, field, field, vector, vector, vector,
                pltpu.VMEM((layers + 2, rows, width), f32), pltpu.VMEM((layers + 2, rows, width), f32),
                pltpu.VMEM((2, layers + 1, 8, long), f32), pltpu.VMEM((2, layers + 1, 8, long), f32),
                pltpu.VMEM((2, 8, 128), f32), pltpu.VMEM((2, 8, 128), f32),
                pltpu.VMEM((1, 128), f32), pltpu.VMEM((n_g, 1, 128), f32), pltpu.VMEM((n_z, 1, 128), f32),
                block, pltpu.VMEM((3, layers, rows, width), f32),
                dma((4,)), dma((2, layers)), dma((2,)), dma((2,)), dma((2, 4)), dma((2, 4)),
                dma((2,)), dma((2,)), dma((2,)), dma((2,)), dma((2, 2, 3)), dma((2, 2, 3)),
                dma, dma, dma, dma, pltpu.SemaphoreType.REGULAR,
            ],
            compiler_params=pltpu.CompilerParams(
                collective_id=0, has_side_effects=True, vmem_limit_bytes=48 * 2**20
            ),
            name="adjoint_step",
        )(record_choice_table, sensitivity_heat, stored_heat, friction_diagonal, stored_motions)

    placed = (
        P("rad", "sub", "dia"),
        P("rad", "sub", "dia"),
        P("rad", "sub", "dia"),
        P(None, None, "rad", "sub", "dia"),
        P("dia"),
    )
    return jax.shard_map(
        shards,
        mesh=mesh,
        in_specs=placed,
        out_specs=(P("rad", "sub", "dia"), P(None, "rad", "sub", "dia")),
        check_vma=False,
    )
```

time: 658 us -> 86.5 us (0.13)
  blocking collectives: 457 us -> 0 us
  starting transfers between devices: 128 us -> 0 us
  Pallas kernels: 0 us -> 79.3 us
  waiting for transfers between devices: 50.3 us -> 0 us
  other arithmetic: 14.8 us -> 0 us
    psum x3 -> x0, blocking collectives: 457 us -> none  [inner_sums(): return lax.psum((first, second), ('dia', 'sub', 'rad'))]
    ppermute x24 -> x0, starting transfers between devices: 128 us -> none  [the longest x12 66.8 us: padded(): lax.ppermute(lax.slice_in_dim(block, block.shape[dim] - width, None, axis...]
    pallas_call x0 -> x1, Pallas kernels: none -> 79.3 us  [shards(): pl.pallas_call(functools.partial(kernel, sizes), out_shape=(jax.ShapeDtyp...]
    ppermute x24 -> x0, waiting for transfers between devices: 50.3 us -> none  [the longest x12 34.7 us: padded(): lax.ppermute(lax.slice_in_dim(block, block.shape[dim] - width, None, axis...]
    reduce_sum x5 -> x0, other arithmetic: 8.43 us -> none  [the longest x3 5.6 us: shards(): jnp.sum(scaled * image)]
  transfers between devices with their start and end apart: 24 -> 0, of which waited for: 12 -> 0; matrix products, arithmetic and copies ran while one was open for 0% -> 0% of each run, Pallas kernels for 0% -> 0%
where the time goes in v1:
time: 86.5 us; the launch traced here: 86.2 us
  Pallas kernels  79.3 us (92%)
  local copies, waits for them, and re-layouts  6.21 us (7%)
    pallas_call x1, Pallas kernels, shards(): pl.pallas_call(functools.partial(kernel, sizes), out_shape=(jax.ShapeDtyp...  79.3 us
    unnamed x12, local copies, waits for them, and re-layouts  6.21 us

profile of v1, /device:TPU:1, one launch (start us, length us, event | category | flops | bytes accessed | tf_op | source)
XLA Modules:
  0.0 86.2 jit_solution(1148054103868507597)
XLA Ops:
  0.6 0.0 copy-start
  0.6 1.1 %copy-done = bf16[2,3,4,16,1024]{4,3,2,1,0:T(8,128)(2,1)S(1)} copy-done((bf16[2,3,4,16,1024]{4,3,2,1,0:T(8,128)(2,1)S(1)}, bf16[2,3,4,16,1024]{4,3,2,1,0:T(8,128)(2,1)}, u32[]{:S(2)}) %copy-start) | copy-done | bytes 786456
  1.8 0.0 copy-start.1
  1.8 0.9 %copy-done.1 = f32[4,16,1024]{2,1,0:T(8,128)S(1)} copy-done((f32[4,16,1024]{2,1,0:T(8,128)S(1)}, f32[4,16,1024]{2,1,0:T(8,128)}, u32[]{:S(2)}) %copy-start.1) | copy-done | bytes 262168
  2.7 0.0 copy-start.2
  2.7 0.9 %copy-done.2 = f32[4,16,1024]{2,1,0:T(8,128)S(1)} copy-done((f32[4,16,1024]{2,1,0:T(8,128)S(1)}, f32[4,16,1024]{2,1,0:T(8,128)}, u32[]{:S(2)}) %copy-start.2) | copy-done | bytes 262168
  3.7 0.0 copy-start.3
  3.7 0.9 %copy-done.3 = f32[4,16,1024]{2,1,0:T(8,128)S(1)} copy-done((f32[4,16,1024]{2,1,0:T(8,128)S(1)}, f32[4,16,1024]{2,1,0:T(8,128)}, u32[]{:S(2)}) %copy-start.3) | copy-done | bytes 262168
  4.6 0.0 copy-start.4
  4.6 0.7 copy-done.4
  5.3 79.3 %adjoint_step.1 = (f32[4,16,1024]{2,1,0:T(8,128)S(1)}, f32[3,4,16,1024]{3,2,1,0:T(8,128)S(1)}) custom-call(s32[2]{0:T(128)S(1)} %copy-done.4, f32[4,16,1024]{2,1,0:T(8,128)S(1)} %copy-done.1, f32[4,16,1024]{2,1,0:T(8,128)S(1)} %copy-done.2, f32[4,16,1024]{2,1,0:T(8,128)S(1)} %copy-done.3, bf16[2,3,4,16,1024]{4,3,2,1,0:T(8,128)(2,1)S(1)} %copy-done), custom_call_target="tpu_custom_call" | custom-call | tf_op jit(solution)/shard_map/adjoint_step/pallas_call | solution.py:471
  84.6 0.7 copy.9
  85.3 0.9 %copy.10 = f32[3,4,16,1024]{3,2,1,0:T(8,128)} copy(f32[3,4,16,1024]{3,2,1,0:T(8,128)S(1)} %get-tuple-element.5) | data formatting | bytes 1572864
Async XLA Ops:
  0.6 1.1 %copy-start = (bf16[2,3,4,16,1024]{4,3,2,1,0:T(8,128)(2,1)S(1)}, bf16[2,3,4,16,1024]{4,3,2,1,0:T(8,128)(2,1)}, u32[]{:S(2)}) copy-start(bf16[2,3,4,16,1024]{4,3,2,1,0:T(8,128)(2,1)} %m_hbm.1) | copy-start | bytes 2359300
  1.8 0.9 %copy-start.1 = (f32[4,16,1024]{2,1,0:T(8,128)S(1)}, f32[4,16,1024]{2,1,0:T(8,128)}, u32[]{:S(2)}) copy-start(f32[4,16,1024]{2,1,0:T(8,128)} %s_hbm.1) | copy-start | bytes 786436
  2.7 0.9 %copy-start.2 = (f32[4,16,1024]{2,1,0:T(8,128)S(1)}, f32[4,16,1024]{2,1,0:T(8,128)}, u32[]{:S(2)}) copy-start(f32[4,16,1024]{2,1,0:T(8,128)} %t_hbm.1) | copy-start | bytes 786436
  3.7 0.9 %copy-start.3 = (f32[4,16,1024]{2,1,0:T(8,128)S(1)}, f32[4,16,1024]{2,1,0:T(8,128)}, u32[]{:S(2)}) copy-start(f32[4,16,1024]{2,1,0:T(8,128)} %f_hbm.1) | copy-start | bytes 786436
  4.6 0.7 copy-start.4

commit v2 on v1

--- a/solution.py
+++ b/solution.py
@@ -44,10 +44,10 @@
 
 
 def kernel(
-    sizes, table, s_hbm, t_hbm, f_hbm, m_hbm, temp_hbm, vel_hbm,
+    sizes, table, s_hbm, t_hbm, f_hbm, m_hbm, adv_hbm, zs_hbm, coef_ref,
     s_v, d_v, m_v, T, Q, I, z0, z1, z2, eu0, ed0,
-    sub_out, sub_in, dia_out, dia_in, mine, plane, column, temp_v, vel_v,
-    load_sem, store_sem, dia_s, dia_r, rad_s, rad_r, sub_s, sub_r, cor_s, cor_r, fwd_s, fwd_r,
+    sub_out, sub_in, dia_out, dia_in, fwd_out, fwd_in, mine, plane, column, temp_v,
+    load_sem, store_sem, dia_s, dia_r, rad_s, rad_r, sub_s, sub_r, cor_s, cor_r, fwd_s, fwd_r, late_s, late_r, edge_s, edge_r,
     plane_s, plane_r, column_s, column_r, relay,
 ):
     n_dia, n_sub, n_rad, n_y, n_core = sizes
@@ -56,7 +56,7 @@
     dia, sub, rad, core, z, g, n_z, n_g, along_z, in_plane = places(sizes)
     reach = max(1, n_z // 4)
     own = pl.ds(H, layers)
-    near = [k for k in range(1, n_z) if min(k, n_z - k) <= reach]
+    near = sorted((k for k in range(1, n_z) if min(k, n_z - k) <= reach), key=lambda k: -min(k, n_z - k))
 
     has_up, has_down = sub < n_sub - 1, sub > 0
     has_above, has_below = rad < n_rad - 1, rad > 0
@@ -65,8 +65,6 @@
     right, left = {"dia": lax.rem(dia + 1, n_dia)}, {"dia": lax.rem(dia + n_dia - 1, n_dia)}
 
     barrier = pltpu.get_barrier_semaphore()
-    for k in near:
-        pl.semaphore_signal(barrier, inc=1, device_id=along_z(k), device_id_type=MESH)
     far_up = jnp.logical_and(core == n_core - 1, has_up)
     far_down = jnp.logical_and(core == 0, has_down)
 
@@ -78,8 +76,8 @@
     def _():
         pl.semaphore_signal(barrier, inc=1, device_id=down, device_id_type=MESH)
 
-    for k in range(1, n_g):
-        pl.semaphore_signal(barrier, inc=1, device_id=in_plane(k), device_id_type=MESH)
+    for k in near:
+        pl.semaphore_signal(barrier, inc=1, device_id=along_z(k), device_id_type=MESH)
 
     loads = [
         pltpu.make_async_copy(s_hbm, s_v, load_sem.at[0]),
@@ -89,6 +87,8 @@
     ]
     for copy in loads:
         copy.start()
+    for k in range(1, n_g):
+        pl.semaphore_signal(barrier, inc=1, device_id=in_plane(k), device_id_type=MESH)
     for copy in loads:
         copy.wait()
 
@@ -117,25 +117,44 @@
 
     lax.fori_loop(0, layers, prepare, 0)
 
-    def pack(columns, edge):
+    def row_plan(way):
+        if way == 0:
+            t, q, i = (rows - 3, rows + 5, 3), (rows - 2, rows + 6, 2), (rows - 1, rows + 7, 1)
+            deep = ((T, rows - 4, rows + 4), (Q, rows - 3, rows + 5), (I, rows - 2, rows + 6))
+            deeper = range(layers // 2, layers)
+        else:
+            t, q, i = (0, rows, 3), (0, rows, 2), (0, rows, 1)
+            deep = ((T, 3, rows + 3), (Q, 2, rows + 2), (I, 1, rows + 1))
+            deeper = range(layers // 2)
+        plan = []
+        for pair in range(layers // 2):
+            plan += [(T, 2 * pair, *t), (T, 2 * pair + 1, *t), (Q, 2 * pair, *q)]
+        for pair in range(layers // 2):
+            plan.append((Q, 2 * pair + 1, *q))
+        plan += [(I, l, *i) for l in range(layers)]
+        for l in deeper:
+            plan += [(ref, l, src, dst, 1) for ref, src, dst in deep]
+        at, placed = 0, []
+        for ref, l, src, dst, count in plan:
+            placed.append((ref, H + l, src, dst, count, at // 8, at % 8))
+            at += count
+        return placed
+
+    def pack(columns):
+        for way in range(2):
+            for ref, L, src, _, count, tile, at in row_plan(way):
+                sub_out[way, tile, at : at + count, columns] = ref[L, src : src + count, columns]
+
+    def pack_edges():
         for l in range(layers):
-            sub_out[0, l, 0:4, columns] = T[H + l, rows - 4 : rows, columns]
-            sub_out[0, l, 4:7, columns] = Q[H + l, rows - 3 : rows, columns]
-            sub_out[0, layers, 2 * l : 2 * l + 2, columns] = I[H + l, rows - 2 : rows, columns]
-            sub_out[1, l, 0:4, columns] = T[H + l, 0:4, columns]
-            sub_out[1, l, 4:7, columns] = Q[H + l, 0:3, columns]
-            sub_out[1, layers, 2 * l : 2 * l + 2, columns] = I[H + l, 0:2, columns]
-            if edge:
-                v = motion(1, l)
-                s = s_v[l]
-                sub_out[0, l, 7:8, columns] = ((0.25 - 0.125 * v) * s)[rows - 1 : rows]
-                sub_out[1, l, 7:8, columns] = ((0.25 + 0.125 * v) * s)[0:1]
-            else:
-                sub_out[0, l, 7:8, columns] = T[H + l, 0:1, columns]
-                sub_out[1, l, 7:8, columns] = T[H + l, 0:1, columns]
+            v = motion(1, l)
+            s = s_v[l]
+            sub_out[0, layers, l : l + 1, :width] = ((0.25 - 0.125 * v) * s)[rows - 1 : rows]
+            sub_out[1, layers, l : l + 1, :width] = ((0.25 + 0.125 * v) * s)[0:1]
 
     main, side = slice(0, width), slice(width, full)
-    pack(main, True)
+    pack(main)
+    pack_edges()
 
     tile_lane = lax.broadcasted_iota(jnp.int32, (1, 128), 1)
     packed = [jnp.zeros((8, 128), jnp.float32), jnp.zeros((8, 128), jnp.float32)]
@@ -170,12 +189,14 @@
 
     @pl.when(jnp.logical_not(has_below))
     def _():
+        fwd_in[0] = jnp.zeros(fwd_in.shape[1:], jnp.float32)
         for ref in (T, Q, I):
             ref[halo_low] = jnp.zeros((H, full_rows, full), jnp.float32)
         ed0[0] = jnp.zeros((rows, width), jnp.float32)
 
     @pl.when(jnp.logical_not(has_above))
     def _():
+        fwd_in[1] = jnp.zeros(fwd_in.shape[1:], jnp.float32)
         for ref in (T, Q, I):
             ref[halo_high] = jnp.zeros((H, full_rows, full), jnp.float32)
         eu0[layers + 1] = jnp.zeros((rows, width), jnp.float32)
@@ -198,13 +219,16 @@
             device_id=device, device_id_type=MESH,
         )
 
-    here, there = slice(0, width), slice(width, full)
     sub_main = [
-        send(sub_out.at[i, :, :, pl.ds(0, width)], sub_in.at[i, :, :, pl.ds(0, width)], sub_s.at[i], sub_r.at[i], to)
+        send(sub_out.at[i, pl.ds(0, layers), :, pl.ds(0, width)], sub_in.at[i, pl.ds(0, layers), :, pl.ds(0, width)], sub_s.at[i], sub_r.at[i], to)
         for i, to in enumerate((up, down))
     ]
     sub_side = [
-        send(sub_out.at[i, :, :, pl.ds(width, 128)], sub_in.at[i, :, :, pl.ds(width, 128)], cor_s.at[i], cor_r.at[i], to)
+        send(sub_out.at[i, pl.ds(0, layers), :, pl.ds(width, 128)], sub_in.at[i, pl.ds(0, layers), :, pl.ds(width, 128)], cor_s.at[i], cor_r.at[i], to)
+        for i, to in enumerate((up, down))
+    ]
+    sub_edge = [
+        send(sub_out.at[i, layers, :, pl.ds(0, width)], sub_in.at[i, layers, :, pl.ds(0, width)], edge_s.at[i], edge_r.at[i], to)
         for i, to in enumerate((up, down))
     ]
     dia_copies = [
@@ -215,26 +239,52 @@
     def slab(ref, first, count, rows_at, lanes_at):
         return ref.at[pl.ds(first, count), pl.ds(*rows_at), pl.ds(*lanes_at)]
 
-    def layer_copies(counts, rows_at, lanes_at, ssem, rsem):
+    def layer_copies(counts, rows_at, lanes_at, ssem, rsem, ahead=0):
         both = [[], []]
         for n, (ref, count) in enumerate(zip((T, Q, I), counts)):
+            skip = (3 - n) if ahead else 0
             both[0].append(send(
-                slab(ref, H + layers - count, count, rows_at, lanes_at),
-                slab(ref, H - count, count, rows_at, lanes_at),
+                slab(ref, H + layers - count - skip, count, rows_at[0], lanes_at),
+                slab(ref, H - count - skip, count, rows_at[0], lanes_at),
                 ssem.at[0, n], rsem.at[0, n], above,
             ))
             both[1].append(send(
-                slab(ref, H, count, rows_at, lanes_at),
-                slab(ref, H + layers, count, rows_at, lanes_at),
+                slab(ref, H + skip, count, rows_at[1], lanes_at),
+                slab(ref, H + layers + skip, count, rows_at[1], lanes_at),
                 ssem.at[1, n], rsem.at[1, n], below,
             ))
         return both
 
-    rad_main = layer_copies((4, 3, 2), (0, rows), (0, width), rad_s, rad_r)
-    rad_main[0].append(send(ed0.at[layers], ed0.at[0], rad_s.at[0, 3], rad_r.at[0, 3], above))
-    rad_main[1].append(send(eu0.at[1], eu0.at[layers + 1], rad_s.at[1, 3], rad_r.at[1, 3], below))
-    rad_side = layer_copies((3, 2, 1), (0, rows), (width, 128), fwd_s.at[0], fwd_r.at[0])
-    rad_rows = layer_copies((3, 2, 1), (rows, 8), (0, full), fwd_s.at[1], fwd_r.at[1])
+    all_rows = ((0, rows), (0, rows))
+    rad_main = layer_copies((3, 2, 1), all_rows, (0, width), rad_s.at[0], rad_r.at[0])
+    rad_deep = layer_copies((1, 1, 1), ((8, 8), (0, 8)), (0, width), rad_s.at[1], rad_r.at[1], 1)
+    rad_side = layer_copies((3, 2, 1), all_rows, (width, 128), fwd_s, fwd_r)
+    rad_edge = [
+        [send(ed0.at[layers], ed0.at[0], edge_s.at[2], edge_r.at[2], above)],
+        [send(eu0.at[1], eu0.at[layers + 1], edge_s.at[3], edge_r.at[3], below)],
+    ]
+    rad_rows = [
+        [send(fwd_out.at[i], fwd_in.at[i], late_s.at[i], late_r.at[i], to)]
+        for i, to in enumerate((above, below))
+    ]
+
+    def corner_plan(way):
+        far = (rows, 1) if way == 0 else (rows + 7, -1)
+        near_side = (rows + 7, -1) if way == 0 else (rows, 1)
+
+        def run(side, depth):
+            return (side[0] if side[1] > 0 else side[0] - depth + 1, depth)
+
+        plan = [(T, 1, *run(far, 3)), (T, 2, *run(far, 2)), (Q, 1, *run(far, 2)), (T, 3, *run(far, 1))]
+        plan += [(T, 1, *run(near_side, 2)), (Q, 2, *run(far, 1)), (I, 1, *run(far, 1))]
+        plan += [(T, 2, *run(near_side, 1)), (Q, 1, *run(near_side, 1))]
+        at, placed = 0, []
+        for ref, depth, first_row, count in plan:
+            src = H + layers - depth if way == 0 else H + depth - 1
+            dst = H - depth if way == 0 else H + layers + depth - 1
+            placed.append((ref, src, dst, first_row, count, at // 8, at % 8))
+            at += count
+        return placed
 
     def start(copies, flag):
         @pl.when(flag)
@@ -258,15 +308,15 @@
     start([sub_main[1]], has_down)
     for copy in dia_copies:
         copy.start()
-    start(rad_main[0], has_above)
-    start(rad_main[1], has_below)
+    for group in (rad_main, rad_deep):
+        start(group[0], has_above)
+        start(group[1], has_below)
 
     for k in sorted({reach, n_z - reach}):
         pl.semaphore_signal(relay, inc=1, device_id=along_z(k), device_id_type=MESH)
 
     for copy in dia_copies:
         copy.wait_recv()
-    eu2_side, ed2_side = [], []
     for l in range(layers):
         for half in range(rows // 8):
             k = l * (rows // 8) + half
@@ -275,20 +325,20 @@
                 from_left = pltpu.roll(dia_in[0], (4 * n + 16 * k) % 128, 1)
                 from_right = pltpu.roll(dia_in[1], (-4 * n - 16 * k) % 128, 1)
                 ref[H + l, group, width:full] = jnp.where(tile_lane < 64, from_right, from_left)
-    pack(side, False)
+    pack(side)
     start([sub_side[0]], has_up)
     start([sub_side[1]], has_down)
     start(rad_side[0], has_above)
     start(rad_side[1], has_below)
+    start([sub_edge[0]], has_up)
+    start([sub_edge[1]], has_down)
+    start(rad_edge[0], has_above)
+    start(rad_edge[1], has_below)
 
     def unpack(columns):
-        for l in range(layers):
-            T[H + l, rows + 4 : rows + 8, columns] = sub_in[0, l, 0:4, columns]
-            Q[H + l, rows + 5 : rows + 8, columns] = sub_in[0, l, 4:7, columns]
-            I[H + l, rows + 6 : rows + 8, columns] = sub_in[0, layers, 2 * l : 2 * l + 2, columns]
-            T[H + l, rows : rows + 4, columns] = sub_in[1, l, 0:4, columns]
-            Q[H + l, rows : rows + 3, columns] = sub_in[1, l, 4:7, columns]
-            I[H + l, rows : rows + 2, columns] = sub_in[1, layers, 2 * l : 2 * l + 2, columns]
+        for way in range(2):
+            for ref, L, _, dst, count, tile, at in row_plan(way):
+                ref[L, dst : dst + count, columns] = sub_in[way, tile, at : at + count, columns]
 
     arrived([sub_main[0]], has_down)
     arrived([sub_main[1]], has_up)
@@ -296,40 +346,45 @@
     arrived([sub_side[0]], has_down)
     arrived([sub_side[1]], has_up)
     unpack(side)
+    for way in range(2):
+        for ref, src, _, row_at, count, tile, at in corner_plan(way):
+            fwd_out[way, tile, at : at + count] = ref[src, row_at : row_at + count]
     start(rad_rows[0], has_above)
     start(rad_rows[1], has_below)
-    for group in (rad_main, rad_side, rad_rows):
+    for group in (rad_main, rad_deep, rad_side, rad_rows):
         arrived(group[0], has_below)
         arrived(group[1], has_above)
-
-    def first(L, carry):
-        t, q = T[L], Q[L]
-        z0[0, L] = q * (T[L + 1] - T[L - 1])
-        z0[1, L] = q * (later(t, 0) - earlier(t, 0))
-        z0[2, L] = q * (later(t, 1) - earlier(t, 1))
-        return carry
-
-    lax.fori_loop(1, layers + 2 * H - 1, first, 0)
-
-    def beside(ref, c, L):
+    for way in range(2):
+        for ref, _, dst, row_at, count, tile, at in corner_plan(way):
+            ref[dst, row_at : row_at + count] = fwd_in[way, tile, at : at + count]
+
+    low_half, high_half, every = slice(0, 8), slice(8, 16), slice(0, full_rows)
+    bottom, top = H - 1, H + layers
+
+    def first_at(L, at):
+        t, q = T[L], Q[L, at]
+        z0[0, L, at] = q * (T[L + 1, at] - T[L - 1, at])
+        z0[1, L, at] = q * (later(t, 0) - earlier(t, 0))[at]
+        z0[2, L, at] = q * (later(t[at], 1) - earlier(t[at], 1))
+
+    def beside(ref, c, L, at):
         x = ref[c, L]
-        rows_sum = later(x, 0) + earlier(x, 0)
-        lanes_sum = later(x, 1) + earlier(x, 1)
-        return ref[c, L + 1] + ref[c, L - 1] + rows_sum + lanes_sum
-
-    def second(L, carry):
+        rows_sum = (later(x, 0) + earlier(x, 0))[at]
+        lanes_sum = later(x[at], 1) + earlier(x[at], 1)
+        return ref[c, L + 1, at] + ref[c, L - 1, at] + rows_sum + lanes_sum
+
+    def next_at(source, target, L, at):
         for c in range(3):
-            z1[c, L] = I[L] * beside(z0, c, L)
-        return carry
-
-    lax.fori_loop(2, layers + 2 * H - 2, second, 0)
-
-    def third(L, carry):
-        for c in range(3):
-            z2[c, L] = I[L] * beside(z1, c, L)
-        return carry
-
-    lax.fori_loop(3, layers + 2 * H - 3, third, 0)
+            target[c, L, at] = I[L, at] * beside(source, c, L, at)
+
+    def over_layers(step, beyond):
+        lax.fori_loop(bottom - beyond + 1, top + beyond, lambda L, carry: (step(L, every), carry)[1], 0)
+        step(bottom - beyond, high_half)
+        step(top + beyond, low_half)
+
+    over_layers(first_at, 2)
+    over_layers(lambda L, at: next_at(z0, z1, L, at), 1)
+    over_layers(lambda L, at: next_at(z1, z2, L, at), 0)
 
     def folded(x):
         total = jnp.zeros((8, 128), jnp.float32)
@@ -338,19 +393,30 @@
                 total = total + x[r : r + 8, w : w + 128]
         return total
 
+    row_at = lax.broadcasted_iota(jnp.int32, (rows, width), 0)
+
     def moments(l, sums):
         L = H + l
         d = d_v[l]
         new = [0.0] * 6
         for c in range(3):
             a, b, e = z0[c, L, :rows, :width], z1[c, L, :rows, :width], z2[c, L, :rows, :width]
-            y = beside(z2, c, L)[:rows, :width]
+            x = z2[c, L]
+            ahead = jnp.where((row_at < 8) | (l < layers - 1), z2[c, L + 1, :rows, :width], 0.0)
+            ahead += jnp.where((row_at < rows - 1) | (l < layers // 2), later(x, 0)[:rows, :width], 0.0)
+            ahead += jnp.where((row_at == 0) & (l >= layers // 2), earlier(x, 0)[:rows, :width], 0.0)
+            ahead += later(x[:rows], 1)[:, :width]
             da, db, de = d * a, d * b, d * e
-            for j, term in enumerate((da * a, da * b, db * b, db * e, de * e, e * y)):
+            for j, term in enumerate((da * a, da * b, db * b, db * e, de * e, e * ahead)):
                 new[j] = new[j] + term
         return tuple(total + folded(x) for total, x in zip(sums, new))
 
-    sums = lax.fori_loop(0, layers, moments, (jnp.zeros((8, 128), jnp.float32),) * 6)
+    sums = list(lax.fori_loop(0, layers, moments, (jnp.zeros((8, 128), jnp.float32),) * 6))
+    for c in range(3):
+        joint = z2[c, H, high_half, :width] * z2[c, bottom, high_half, :width]
+        for w in range(0, width, 128):
+            sums[5] = sums[5] + joint[:, w : w + 128]
+    sums[5] = 2.0 * sums[5]
 
     row = jnp.zeros((1, 128), jnp.float32)
     for j in range(6):
@@ -364,6 +430,10 @@
         return send(slots.at[pl.ds(0, count - 1)], slots.at[pl.ds(0, count - 1)], ssem, rsem, peer(1))
 
     copies = exchange(row, plane, n_g, g, in_plane, plane_s, plane_r, range(1, n_g))
+    stores = [
+        pltpu.make_async_copy(ref.at[:, own, pl.ds(0, rows), pl.ds(0, width)], zs_hbm.at[k], store_sem.at[k])
+        for k, ref in enumerate((z0, z1, z2))
+    ]
     copies.wait_recv()
     copies.wait_send()
     row = jnp.sum(plane[...], axis=0)
@@ -371,14 +441,20 @@
     pl.semaphore_wait(relay, len({reach, n_z - reach}))
     copies = exchange(row, column, n_z, z, along_z, column_s, column_r, far_first)
 
+    for copy in stores:
+        copy.start()
+    arrived([sub_edge[0]], has_down)
+    arrived([sub_edge[1]], has_up)
+    arrived(rad_edge[0], has_below)
+    arrived(rad_edge[1], has_above)
+
     def advect(l, carry):
         s = s_v[l]
         v1, v2 = motion(1, l), motion(2, l)
-        row_at = lax.broadcasted_iota(jnp.int32, (rows, width), 0)
         total = -0.5 * s + eu0[l + 2] + ed0[l]
         u, w = (0.25 + 0.125 * v1) * s, (0.25 - 0.125 * v1) * s
-        total = total + jnp.where(row_at == rows - 1, sub_in[1, l, 7:8, :width], later(u, 0))
-        total = total + jnp.where(row_at == 0, sub_in[0, l, 7:8, :width], earlier(w, 0))
+        total = total + jnp.where(row_at == rows - 1, sub_in[1, layers, pl.ds(l, 1), :width], later(u, 0))
+        total = total + jnp.where(row_at == 0, sub_in[0, layers, pl.ds(l, 1), :width], earlier(w, 0))
         u, w = (0.25 + 0.125 * v2) * s, (0.25 - 0.125 * v2) * s
         temp_v[l] = total + later(u, 1) + earlier(w, 1)
         return carry
@@ -404,6 +480,18 @@
             from_right = pltpu.roll(dia_in[1], (127 - 12 - 16 * k) % 128, 1)
             temp_v[l, group, low] += jnp.where(tile_lane == 0, from_left - w, 0.0)
             temp_v[l, group, high] += jnp.where(tile_lane == 127, from_right - u, 0.0)
+
+    stores.append(pltpu.make_async_copy(temp_v, adv_hbm, store_sem.at[3]))
+    stores[3].start()
+    left_here([sub_main[0], sub_side[0], sub_edge[0]], has_up)
+    left_here([sub_main[1], sub_side[1], sub_edge[1]], has_down)
+    for copy in dia_copies:
+        copy.wait_send()
+    for group in (rad_main, rad_deep, rad_side, rad_rows, rad_edge):
+        left_here(group[0], has_above)
+        left_here(group[1], has_below)
+    for copy in stores:
+        copy.wait()
 
     copies.wait_recv()
     copies.wait_send()
@@ -428,28 +516,20 @@
     alpha2 = step(p2)
     c0, c1, c2 = (alpha0 * x + alpha1 * y + alpha2 * w for x, y, w in zip(p0, p1, p2))
 
-    stores = []
-    for l in range(layers):
-        stores.append(pltpu.make_async_copy(vel_v.at[:, l], vel_hbm.at[:, l], store_sem.at[0, l]))
-        stores.append(pltpu.make_async_copy(temp_v.at[l], temp_hbm.at[l], store_sem.at[1, l]))
-        for c in range(3):
-            at = (c, H + l, slice(0, rows), slice(0, width))
-            velocity = c0 * z0[at] + c1 * z1[at] + c2 * z2[at]
-            vel_v[c, l] = velocity
-            if c == 0:
-                temp_v[l] = temp_v[l] + 4.0 * velocity
-        stores[-2].start()
-        stores[-1].start()
-
-    left_here([sub_main[0], sub_side[0]], has_up)
-    left_here([sub_main[1], sub_side[1]], has_down)
-    for copy in dia_copies:
-        copy.wait_send()
-    for group in (rad_main, rad_side, rad_rows):
-        left_here(group[0], has_above)
-        left_here(group[1], has_below)
-    for copy in stores:
-        copy.wait()
+    wide = jnp.zeros((8, 128), jnp.float32)
+    row_of = lax.broadcasted_iota(jnp.int32, (8, 128), 0)
+    for n, value in enumerate((c0, c1, c2)):
+        wide = jnp.where(row_of == n, value, wide)
+    coef_ref[...] = wide
+
+
+def finish(coef_ref, adv_ref, zs_ref, temp_ref, vel_ref):
+    c0, c1, c2 = (coef_ref[n : n + 1, 0:1] for n in range(3))
+    for c in range(3):
+        velocity = c0 * zs_ref[0, c, 0] + c1 * zs_ref[1, c, 0] + c2 * zs_ref[2, c, 0]
+        vel_ref[c, 0] = velocity
+        if c == 0:
+            temp_ref[0] = adv_ref[0] + 4.0 * velocity
 
 
 def solution(mesh):
@@ -467,32 +547,52 @@
         field = pltpu.VMEM((tall, wide, long), f32)
         vector = pltpu.VMEM((3, tall, wide, long), f32)
         dma = pltpu.SemaphoreType.DMA
-        anywhere = pl.BlockSpec(memory_space=pl.ANY)
-        return pl.pallas_call(
+        in_hbm = pl.BlockSpec(memory_space=pltpu.HBM)
+        advected, zs, coefficients = pl.pallas_call(
             functools.partial(kernel, sizes),
             out_shape=(
                 jax.ShapeDtypeStruct((layers, rows, width), f32),
-                jax.ShapeDtypeStruct((3, layers, rows, width), f32),
+                jax.ShapeDtypeStruct((3, 3, layers, rows, width), f32),
+                jax.ShapeDtypeStruct((8, 128), f32),
             ),
-            in_specs=[pl.BlockSpec(memory_space=pltpu.SMEM)] + [anywhere] * 4,
-            out_specs=(anywhere, anywhere),
+            in_specs=[pl.BlockSpec(memory_space=pltpu.SMEM)] + [in_hbm] * 4,
+            out_specs=(in_hbm, in_hbm, pl.BlockSpec(memory_space=pltpu.VMEM)),
             scratch_shapes=[
                 block, block, pltpu.VMEM(stored_motions.shape, stored_motions.dtype),
                 field, field, field, vector, vector, vector,
                 pltpu.VMEM((layers + 2, rows, width), f32), pltpu.VMEM((layers + 2, rows, width), f32),
                 pltpu.VMEM((2, layers + 1, 8, long), f32), pltpu.VMEM((2, layers + 1, 8, long), f32),
                 pltpu.VMEM((2, 8, 128), f32), pltpu.VMEM((2, 8, 128), f32),
+                pltpu.VMEM((2, 2, 8, long), f32), pltpu.VMEM((2, 2, 8, long), f32),
                 pltpu.VMEM((1, 128), f32), pltpu.VMEM((n_g, 1, 128), f32), pltpu.VMEM((n_z, 1, 128), f32),
-                block, pltpu.VMEM((3, layers, rows, width), f32),
-                dma((4,)), dma((2, layers)), dma((2,)), dma((2,)), dma((2, 4)), dma((2, 4)),
-                dma((2,)), dma((2,)), dma((2,)), dma((2,)), dma((2, 2, 3)), dma((2, 2, 3)),
+                block,
+                dma((4,)), dma((4,)), dma((2,)), dma((2,)), dma((2, 2, 3)), dma((2, 2, 3)),
+                dma((2,)), dma((2,)), dma((2,)), dma((2,)), dma((2, 3)), dma((2, 3)),
+                dma((2,)), dma((2,)), dma((4,)), dma((4,)),
                 dma, dma, dma, dma, pltpu.SemaphoreType.REGULAR,
             ],
             compiler_params=pltpu.CompilerParams(
-                collective_id=0, has_side_effects=True, vmem_limit_bytes=48 * 2**20
+                collective_id=0, has_side_effects=True, vmem_limit_bytes=60 * 2**20
             ),
             name="adjoint_step",
         )(record_choice_table, sensitivity_heat, stored_heat, friction_diagonal, stored_motions)
+        layer = pl.BlockSpec((1, rows, width), lambda l: (l, 0, 0))
+        return pl.pallas_call(
+            finish,
+            grid=(layers,),
+            out_shape=(
+                jax.ShapeDtypeStruct((layers, rows, width), f32),
+                jax.ShapeDtypeStruct((3, layers, rows, width), f32),
+            ),
+            in_specs=[
+                pl.BlockSpec((8, 128), lambda l: (0, 0)),
+                layer,
+                pl.BlockSpec((3, 3, 1, rows, width), lambda l: (0, 0, l, 0, 0)),
+            ],
+            out_specs=(layer, pl.BlockSpec((3, 1, rows, width), lambda l: (0, l, 0, 0))),
+            compiler_params=pltpu.CompilerParams(vmem_limit_bytes=60 * 2**20),
+            name="finish",
+        )(coefficients, advected, zs)
 
     placed = (
         P("rad", "sub", "dia"),

time: 86.5 us -> 78.7 us (0.910)
  local copies, waits for them, and re-layouts: 6.21 us -> 0 us
  Pallas kernels: 79.3 us -> 77.8 us
    unnamed x12 -> x0, local copies, waits for them, and re-layouts: 6.21 us -> none
    pallas_call x1, Pallas kernels: 79.3 us -> 74.1 us  [shards(): pl.pallas_call(functools.partial(kernel, sizes), out_shape=(jax.ShapeDtyp...]
    pallas_call x0 -> x1, Pallas kernels: none -> 3.77 us  [shards(): pl.pallas_call(finish, grid=(layers,), out_shape=(jax.ShapeDtypeStruct((l...]
where the time goes in v2:
time: 78.7 us; the launch traced here: 78.5 us
  Pallas kernels  77.8 us (99%)
    pallas_call x1, Pallas kernels, shards(): pl.pallas_call(functools.partial(kernel, sizes), out_shape=(jax.ShapeDtyp...  74.1 us
    pallas_call x1, Pallas kernels, shards(): pl.pallas_call(finish, grid=(layers,), out_shape=(jax.ShapeDtypeStruct((l...  3.77 us

profile of v2, /device:TPU:1, one launch (start us, length us, event | category | flops | bytes accessed | tf_op | source)
XLA Modules:
  0.0 78.5 jit_solution(10679726550382884717)
XLA Ops:
  0.6 74.1 %adjoint_step.1 = (f32[4,16,1024]{2,1,0:T(8,128)}, f32[3,3,4,16,1024]{4,3,2,1,0:T(8,128)}, f32[8,128]{1,0:T(8,128)}) custom-call(s32[2]{0:T(128)} %table.1, f32[4,16,1024]{2,1,0:T(8,128)} %s_hbm.1, f32[4,16,1024]{2,1,0:T(8,128)} %t_hbm.1, f32[4,16,1024]{2,1,0:T(8,128)} %f_hbm.1, bf16[2,3,4,16,1024]{4,3,2,1,0:T(8,128)(2,1)} %m_hbm.1), custom_call_target="tpu_custom_call" | custom-call | tf_op jit(solution)/shard_map/adjoint_step/pallas_call | solution.py:551
  74.7 3.8 %finish.1 = (f32[4,16,1024]{2,1,0:T(8,128)}, f32[3,4,16,1024]{3,2,1,0:T(8,128)}) custom-call(f32[8,128]{1,0:T(8,128)} %get-tuple-element.5.coef_ref, f32[4,16,1024]{2,1,0:T(8,128)} %get-tuple-element.6.adv_ref, f32[3,3,4,16,1024]{4,3,2,1,0:T(8,128)} %get-tuple-element.7.zs_ref), custom_call_target="tpu_custom_call" | custom-call | tf_op jit(solution)/shard_map/finish/pallas_call | solution.py:580

commit v3 on v2

--- a/solution.py
+++ b/solution.py
@@ -224,7 +224,7 @@
         for i, to in enumerate((up, down))
     ]
     sub_side = [
-        send(sub_out.at[i, pl.ds(0, layers), :, pl.ds(width, 128)], sub_in.at[i, pl.ds(0, layers), :, pl.ds(width, 128)], cor_s.at[i], cor_r.at[i], to)
+        send(sub_out.at[i, pl.ds(0, layers - 1), :, pl.ds(width, 128)], sub_in.at[i, pl.ds(0, layers - 1), :, pl.ds(width, 128)], cor_s.at[i], cor_r.at[i], to)
         for i, to in enumerate((up, down))
     ]
     sub_edge = [
@@ -340,6 +340,50 @@
             for ref, L, _, dst, count, tile, at in row_plan(way):
                 ref[L, dst : dst + count, columns] = sub_in[way, tile, at : at + count, columns]
 
+    low_half, high_half, every = slice(0, 8), slice(8, 16), slice(0, full_rows)
+    inner, outer = slice(0, rows), slice(rows, full_rows)
+    bottom, top = H - 1, H + layers
+
+    def across_layers(L, at):
+        z0[0, L, at] = Q[L, at] * (T[L + 1, at] - T[L - 1, at])
+
+    def across_rows(L, at):
+        t = T[L]
+        z0[1, L, at] = Q[L, at] * (later(t, 0) - earlier(t, 0))[at]
+
+    def across_columns(L, at):
+        t = T[L, at]
+        z0[2, L, at] = Q[L, at] * (later(t, 1) - earlier(t, 1))
+
+    def column_sum(ref, c, L, at):
+        x = ref[c, L, at]
+        return later(x, 1) + earlier(x, 1)
+
+    def other_sum(ref, c, L, at):
+        x = ref[c, L]
+        return ref[c, L + 1, at] + ref[c, L - 1, at] + (later(x, 0) + earlier(x, 0))[at]
+
+    def over_layers(step, beyond, at, deep=True):
+        lax.fori_loop(bottom - beyond + 1, top + beyond, lambda L, carry: (step(L, at), carry)[1], 0)
+        if deep:
+            step(bottom - beyond, high_half)
+            step(top + beyond, low_half)
+
+    for group in (rad_main, rad_deep, rad_side):
+        arrived(group[0], has_below)
+        arrived(group[1], has_above)
+
+    def early(L, at):
+        across_layers(L, at)
+        across_columns(L, at)
+
+    def early_sums(L, at):
+        for c in (0, 2):
+            z1[c, L, at] = column_sum(z0, c, L, at)
+
+    over_layers(early, 2, inner)
+    over_layers(early_sums, 1, inner)
+
     arrived([sub_main[0]], has_down)
     arrived([sub_main[1]], has_up)
     unpack(main)
@@ -351,40 +395,42 @@
             fwd_out[way, tile, at : at + count] = ref[src, row_at : row_at + count]
     start(rad_rows[0], has_above)
     start(rad_rows[1], has_below)
-    for group in (rad_main, rad_deep, rad_side, rad_rows):
-        arrived(group[0], has_below)
-        arrived(group[1], has_above)
+
+    def late(L, carry):
+        across_layers(L, outer)
+        across_columns(L, outer)
+        across_rows(L, every)
+        return carry
+
+    lax.fori_loop(H + 1, H + layers - 1, late, 0)
+    arrived(rad_rows[0], has_below)
+    arrived(rad_rows[1], has_above)
     for way in range(2):
         for ref, _, dst, row_at, count, tile, at in corner_plan(way):
             ref[dst, row_at : row_at + count] = fwd_in[way, tile, at : at + count]
 
-    low_half, high_half, every = slice(0, 8), slice(8, 16), slice(0, full_rows)
-    bottom, top = H - 1, H + layers
-
-    def first_at(L, at):
-        t, q = T[L], Q[L, at]
-        z0[0, L, at] = q * (T[L + 1, at] - T[L - 1, at])
-        z0[1, L, at] = q * (later(t, 0) - earlier(t, 0))[at]
-        z0[2, L, at] = q * (later(t[at], 1) - earlier(t[at], 1))
-
-    def beside(ref, c, L, at):
-        x = ref[c, L]
-        rows_sum = (later(x, 0) + earlier(x, 0))[at]
-        lanes_sum = later(x[at], 1) + earlier(x[at], 1)
-        return ref[c, L + 1, at] + ref[c, L - 1, at] + rows_sum + lanes_sum
-
-    def next_at(source, target, L, at):
+    lax.fori_loop(bottom - 1, H + 1, late, 0)
+    lax.fori_loop(H + layers - 1, top + 2, late, 0)
+    across_rows(bottom - 2, high_half)
+    across_rows(top + 2, low_half)
+
+    def second(L, at):
+        for c in (0, 2):
+            z1[c, L, at] = I[L, at] * (z1[c, L, at] + other_sum(z0, c, L, at))
+        z1[1, L, at] = I[L, at] * (column_sum(z0, 1, L, at) + other_sum(z0, 1, L, at))
+
+    def second_outer(L, at):
+        for c in (0, 2):
+            z1[c, L, at] = I[L, at] * (column_sum(z0, c, L, at) + other_sum(z0, c, L, at))
+        z1[1, L, at] = I[L, at] * (column_sum(z0, 1, L, at) + other_sum(z0, 1, L, at))
+
+    def third(L, at):
         for c in range(3):
-            target[c, L, at] = I[L, at] * beside(source, c, L, at)
-
-    def over_layers(step, beyond):
-        lax.fori_loop(bottom - beyond + 1, top + beyond, lambda L, carry: (step(L, every), carry)[1], 0)
-        step(bottom - beyond, high_half)
-        step(top + beyond, low_half)
-
-    over_layers(first_at, 2)
-    over_layers(lambda L, at: next_at(z0, z1, L, at), 1)
-    over_layers(lambda L, at: next_at(z1, z2, L, at), 0)
+            z2[c, L, at] = I[L, at] * (column_sum(z1, c, L, at) + other_sum(z1, c, L, at))
+
+    over_layers(second, 1, inner)
+    over_layers(second_outer, 1, outer, False)
+    over_layers(third, 0, every)
 
     def folded(x):
         total = jnp.zeros((8, 128), jnp.float32)
@@ -523,13 +569,31 @@
     coef_ref[...] = wide
 
 
-def finish(coef_ref, adv_ref, zs_ref, temp_ref, vel_ref):
-    c0, c1, c2 = (coef_ref[n : n + 1, 0:1] for n in range(3))
-    for c in range(3):
-        velocity = c0 * zs_ref[0, c, 0] + c1 * zs_ref[1, c, 0] + c2 * zs_ref[2, c, 0]
-        vel_ref[c, 0] = velocity
-        if c == 0:
-            temp_ref[0] = adv_ref[0] + 4.0 * velocity
+def finish(coef_hbm, adv_hbm, zs_hbm, temp_hbm, vel_hbm, coef, adv, zs, temp, vel, load_sem, store_sem):
+    layers = adv.shape[0]
+    loads, stores = [pltpu.make_async_copy(coef_hbm, coef, load_sem.at[2, 0])], []
+    loads[0].start()
+    for l in range(layers):
+        loads.append(pltpu.make_async_copy(zs_hbm.at[:, :, l], zs.at[:, :, l], load_sem.at[0, l]))
+        loads.append(pltpu.make_async_copy(adv_hbm.at[l], adv.at[l], load_sem.at[1, l]))
+        stores.append(pltpu.make_async_copy(vel.at[:, l], vel_hbm.at[:, l], store_sem.at[0, l]))
+        stores.append(pltpu.make_async_copy(temp.at[l], temp_hbm.at[l], store_sem.at[1, l]))
+        loads[-2].start()
+        loads[-1].start()
+    loads[0].wait()
+    c0, c1, c2 = (coef[n : n + 1, 0:1] for n in range(3))
+    for l in range(layers):
+        loads[2 * l + 1].wait()
+        loads[2 * l + 2].wait()
+        for c in range(3):
+            velocity = c0 * zs[0, c, l] + c1 * zs[1, c, l] + c2 * zs[2, c, l]
+            vel[c, l] = velocity
+            if c == 0:
+                temp[l] = adv[l] + 4.0 * velocity
+        stores[2 * l].start()
+        stores[2 * l + 1].start()
+    for copy in stores:
+        copy.wait()
 
 
 def solution(mesh):
@@ -576,20 +640,18 @@
             ),
             name="adjoint_step",
         )(record_choice_table, sensitivity_heat, stored_heat, friction_diagonal, stored_motions)
-        layer = pl.BlockSpec((1, rows, width), lambda l: (l, 0, 0))
         return pl.pallas_call(
             finish,
-            grid=(layers,),
             out_shape=(
                 jax.ShapeDtypeStruct((layers, rows, width), f32),
                 jax.ShapeDtypeStruct((3, layers, rows, width), f32),
             ),
-            in_specs=[
-                pl.BlockSpec((8, 128), lambda l: (0, 0)),
-                layer,
-                pl.BlockSpec((3, 3, 1, rows, width), lambda l: (0, 0, l, 0, 0)),
+            in_specs=[in_hbm] * 3,
+            out_specs=(in_hbm, in_hbm),
+            scratch_shapes=[
+                pltpu.VMEM((8, 128), f32), block, pltpu.VMEM((3, 3, layers, rows, width), f32),
+                block, pltpu.VMEM((3, layers, rows, width), f32), dma((3, layers)), dma((2, layers)),
             ],
-            out_specs=(layer, pl.BlockSpec((3, 1, rows, width), lambda l: (0, l, 0, 0))),
             compiler_params=pltpu.CompilerParams(vmem_limit_bytes=60 * 2**20),
             name="finish",
         )(coefficients, advected, zs)

time: 78.7 us -> 76.5 us (0.972)
  Pallas kernels: 77.8 us -> 75.7 us
    pallas_call x1, Pallas kernels: 3.77 us -> 2.57 us  [shards(): pl.pallas_call(finish, out_shape=(jax.ShapeDtypeStruct((layers, rows, wid...]
    pallas_call x1, Pallas kernels: 74.1 us -> 73.1 us  [shards(): pl.pallas_call(functools.partial(kernel, sizes), out_shape=(jax.ShapeDtyp...]
where the time goes in v3:
time: 76.5 us; the launch traced here: 76.3 us
  Pallas kernels  75.7 us (99%)
    pallas_call x1, Pallas kernels, shards(): pl.pallas_call(functools.partial(kernel, sizes), out_shape=(jax.ShapeDtyp...  73.1 us
    pallas_call x1, Pallas kernels, shards(): pl.pallas_call(finish, out_shape=(jax.ShapeDtypeStruct((layers, rows, wid...  2.57 us

profile of v3, /device:TPU:1, one launch (start us, length us, event | category | flops | bytes accessed | tf_op | source)
XLA Modules:
  0.0 76.3 jit_solution(2469229034917024980)
XLA Ops:
  0.6 73.1 %adjoint_step.1 = (f32[4,16,1024]{2,1,0:T(8,128)}, f32[3,3,4,16,1024]{4,3,2,1,0:T(8,128)}, f32[8,128]{1,0:T(8,128)}) custom-call(s32[2]{0:T(128)} %table.1, f32[4,16,1024]{2,1,0:T(8,128)} %s_hbm.1, f32[4,16,1024]{2,1,0:T(8,128)} %t_hbm.1, f32[4,16,1024]{2,1,0:T(8,128)} %f_hbm.1, bf16[2,3,4,16,1024]{4,3,2,1,0:T(8,128)(2,1)} %m_hbm.1), custom_call_target="tpu_custom_call" | custom-call | tf_op jit(solution)/shard_map/adjoint_step/pallas_call | solution.py:615
  73.7 2.6 %finish.1 = (f32[4,16,1024]{2,1,0:T(8,128)}, f32[3,4,16,1024]{3,2,1,0:T(8,128)}) custom-call(f32[8,128]{1,0:T(8,128)} %get-tuple-element.5.coef_hbm, f32[4,16,1024]{2,1,0:T(8,128)} %get-tuple-element.6.adv_hbm, f32[3,3,4,16,1024]{4,3,2,1,0:T(8,128)} %get-tuple-element.7.zs_hbm), custom_call_target="tpu_custom_call" | custom-call | tf_op jit(solution)/shard_map/finish/pallas_call | solution.py:643

commit v4 on v3

--- a/solution.py
+++ b/solution.py
@@ -46,7 +46,7 @@
 def kernel(
     sizes, table, s_hbm, t_hbm, f_hbm, m_hbm, adv_hbm, zs_hbm, coef_ref,
     s_v, d_v, m_v, T, Q, I, z0, z1, z2, eu0, ed0,
-    sub_out, sub_in, dia_out, dia_in, fwd_out, fwd_in, mine, plane, column, temp_v,
+    sub_out, sub_in, dia_out, dia_in, fwd_out, fwd_in, side_out, side_in, mine, plane, column, temp_v,
     load_sem, store_sem, dia_s, dia_r, rad_s, rad_r, sub_s, sub_r, cor_s, cor_r, fwd_s, fwd_r, late_s, late_r, edge_s, edge_r,
     plane_s, plane_r, column_s, column_r, relay,
 ):
@@ -204,10 +204,12 @@
     @pl.when(jnp.logical_not(has_down))
     def _():
         sub_in[0] = jnp.zeros(sub_in.shape[1:], jnp.float32)
+        side_in[0] = jnp.zeros(side_in.shape[1:], jnp.float32)
 
     @pl.when(jnp.logical_not(has_up))
     def _():
         sub_in[1] = jnp.zeros(sub_in.shape[1:], jnp.float32)
+        side_in[1] = jnp.zeros(side_in.shape[1:], jnp.float32)
 
     pl.semaphore_wait(
         barrier, len(near) + n_g - 1 + far_up.astype(jnp.int32) + far_down.astype(jnp.int32)
@@ -219,12 +221,16 @@
             device_id=device, device_id_type=MESH,
         )
 
+    chunks = (pl.ds(0, width // 2), pl.ds(width // 2, width // 2))
     sub_main = [
-        send(sub_out.at[i, pl.ds(0, layers), :, pl.ds(0, width)], sub_in.at[i, pl.ds(0, layers), :, pl.ds(0, width)], sub_s.at[i], sub_r.at[i], to)
+        [
+            send(sub_out.at[i, pl.ds(0, layers), :, at], sub_in.at[i, pl.ds(0, layers), :, at], sub_s.at[i, j], sub_r.at[i, j], to)
+            for j, at in enumerate(chunks)
+        ]
         for i, to in enumerate((up, down))
     ]
     sub_side = [
-        send(sub_out.at[i, pl.ds(0, layers - 1), :, pl.ds(width, 128)], sub_in.at[i, pl.ds(0, layers - 1), :, pl.ds(width, 128)], cor_s.at[i], cor_r.at[i], to)
+        send(side_out.at[i], side_in.at[i], cor_s.at[i], cor_r.at[i], to)
         for i, to in enumerate((up, down))
     ]
     sub_edge = [
@@ -263,8 +269,12 @@
         [send(ed0.at[layers], ed0.at[0], edge_s.at[2], edge_r.at[2], above)],
         [send(eu0.at[1], eu0.at[layers + 1], edge_s.at[3], edge_r.at[3], below)],
     ]
+    parts = (pl.ds(0, width // 2), pl.ds(width // 2, full - width // 2))
     rad_rows = [
-        [send(fwd_out.at[i], fwd_in.at[i], late_s.at[i], late_r.at[i], to)]
+        [
+            send(fwd_out.at[i, :, :, at], fwd_in.at[i, :, :, at], late_s.at[i, j], late_r.at[i, j], to)
+            for j, at in enumerate(parts)
+        ]
         for i, to in enumerate((above, below))
     ]
 
@@ -304,8 +314,9 @@
             for copy in copies:
                 copy.wait_send()
 
-    start([sub_main[0]], has_up)
-    start([sub_main[1]], has_down)
+    for j in range(2):
+        start([sub_main[0][j]], has_up)
+        start([sub_main[1][j]], has_down)
     for copy in dia_copies:
         copy.start()
     for group in (rad_main, rad_deep):
@@ -326,6 +337,12 @@
                 from_right = pltpu.roll(dia_in[1], (-4 * n - 16 * k) % 128, 1)
                 ref[H + l, group, width:full] = jnp.where(tile_lane < 64, from_right, from_left)
     pack(side)
+    for way in range(2):
+        tile = sub_out[way, 0, :, side]
+        for k in range(1, layers - 1):
+            low = 8 * k - 4
+            tile = jnp.where((tile_lane >= low) & (tile_lane < low + 8), pltpu.roll(sub_out[way, k, :, side], 8 * k, 1), tile)
+        side_out[way] = tile
     start([sub_side[0]], has_up)
     start([sub_side[1]], has_down)
     start(rad_side[0], has_above)
@@ -369,6 +386,18 @@
             step(bottom - beyond, high_half)
             step(top + beyond, low_half)
 
+    def forward(columns, j):
+        for way in range(2):
+            for ref, src, _, row_at, count, tile, at in corner_plan(way):
+                fwd_out[way, tile, at : at + count, columns] = ref[src, row_at : row_at + count, columns]
+        start([rad_rows[0][j]], has_above)
+        start([rad_rows[1][j]], has_below)
+
+    arrived([sub_main[0][0]], has_down)
+    arrived([sub_main[1][0]], has_up)
+    unpack(slice(0, width // 2))
+    forward(slice(0, width // 2), 0)
+
     for group in (rad_main, rad_deep, rad_side):
         arrived(group[0], has_below)
         arrived(group[1], has_above)
@@ -384,17 +413,16 @@
     over_layers(early, 2, inner)
     over_layers(early_sums, 1, inner)
 
-    arrived([sub_main[0]], has_down)
-    arrived([sub_main[1]], has_up)
-    unpack(main)
+    arrived([sub_main[0][1]], has_down)
+    arrived([sub_main[1][1]], has_up)
+    unpack(slice(width // 2, width))
     arrived([sub_side[0]], has_down)
     arrived([sub_side[1]], has_up)
+    for way in range(2):
+        for k in range(layers - 1):
+            sub_in[way, k, :, side] = pltpu.roll(side_in[way], (-8 * k) % 128, 1)
     unpack(side)
-    for way in range(2):
-        for ref, src, _, row_at, count, tile, at in corner_plan(way):
-            fwd_out[way, tile, at : at + count] = ref[src, row_at : row_at + count]
-    start(rad_rows[0], has_above)
-    start(rad_rows[1], has_below)
+    forward(slice(width // 2, full), 1)
 
     def late(L, carry):
         across_layers(L, outer)
@@ -468,24 +496,28 @@
     for j in range(6):
         row = jnp.where(tile_lane == j, jnp.sum(sums[j], keepdims=True), row)
 
-    def exchange(value, slots, count, index, peer, ssem, rsem, order):
-        mine[...] = value
+    def exchange(value, turn, slots, count, index, peer, ssem, rsem, order):
+        mine[turn] = value
         slots[index] = value
         for k in order:
-            send(mine, slots.at[index], ssem, rsem, peer(k)).start()
+            send(mine.at[turn], slots.at[index], ssem, rsem, peer(k)).start()
         return send(slots.at[pl.ds(0, count - 1)], slots.at[pl.ds(0, count - 1)], ssem, rsem, peer(1))
 
-    copies = exchange(row, plane, n_g, g, in_plane, plane_s, plane_r, range(1, n_g))
+    def hops(k):
+        across, along = k // (n_y * n_core), (k // n_core) % n_y
+        return min(across, n_rad - across) + min(along, n_y - along)
+
+    far_in_plane = sorted(range(1, n_g), key=lambda k: -hops(k))
+    in_plane_copies = exchange(row, 0, plane, n_g, g, in_plane, plane_s, plane_r, far_in_plane)
     stores = [
         pltpu.make_async_copy(ref.at[:, own, pl.ds(0, rows), pl.ds(0, width)], zs_hbm.at[k], store_sem.at[k])
         for k, ref in enumerate((z0, z1, z2))
     ]
-    copies.wait_recv()
-    copies.wait_send()
+    in_plane_copies.wait_recv()
     row = jnp.sum(plane[...], axis=0)
     far_first = sorted(range(1, n_z), key=lambda k: -min(k, n_z - k))
     pl.semaphore_wait(relay, len({reach, n_z - reach}))
-    copies = exchange(row, column, n_z, z, along_z, column_s, column_r, far_first)
+    copies = exchange(row, 1, column, n_z, z, along_z, column_s, column_r, far_first)
 
     for copy in stores:
         copy.start()
@@ -529,8 +561,8 @@
 
     stores.append(pltpu.make_async_copy(temp_v, adv_hbm, store_sem.at[3]))
     stores[3].start()
-    left_here([sub_main[0], sub_side[0], sub_edge[0]], has_up)
-    left_here([sub_main[1], sub_side[1], sub_edge[1]], has_down)
+    left_here(sub_main[0] + [sub_side[0], sub_edge[0]], has_up)
+    left_here(sub_main[1] + [sub_side[1], sub_edge[1]], has_down)
     for copy in dia_copies:
         copy.wait_send()
     for group in (rad_main, rad_deep, rad_side, rad_rows, rad_edge):
@@ -538,6 +570,7 @@
         left_here(group[1], has_below)
     for copy in stores:
         copy.wait()
+    in_plane_copies.wait_send()
 
     copies.wait_recv()
     copies.wait_send()
@@ -628,11 +661,11 @@
                 pltpu.VMEM((2, layers + 1, 8, long), f32), pltpu.VMEM((2, layers + 1, 8, long), f32),
                 pltpu.VMEM((2, 8, 128), f32), pltpu.VMEM((2, 8, 128), f32),
                 pltpu.VMEM((2, 2, 8, long), f32), pltpu.VMEM((2, 2, 8, long), f32),
-                pltpu.VMEM((1, 128), f32), pltpu.VMEM((n_g, 1, 128), f32), pltpu.VMEM((n_z, 1, 128), f32),
+                pltpu.VMEM((2, 8, 128), f32), pltpu.VMEM((2, 8, 128), f32), pltpu.VMEM((2, 1, 128), f32), pltpu.VMEM((n_g, 1, 128), f32), pltpu.VMEM((n_z, 1, 128), f32),
                 block,
                 dma((4,)), dma((4,)), dma((2,)), dma((2,)), dma((2, 2, 3)), dma((2, 2, 3)),
-                dma((2,)), dma((2,)), dma((2,)), dma((2,)), dma((2, 3)), dma((2, 3)),
-                dma((2,)), dma((2,)), dma((4,)), dma((4,)),
+                dma((2, 2)), dma((2, 2)), dma((2,)), dma((2,)), dma((2, 3)), dma((2, 3)),
+                dma((2, 2)), dma((2, 2)), dma((4,)), dma((4,)),
                 dma, dma, dma, dma, pltpu.SemaphoreType.REGULAR,
             ],
             compiler_params=pltpu.CompilerParams(

time: 76.5 us -> 75.4 us (0.986)
  Pallas kernels: 75.7 us -> 74.5 us
    pallas_call x1, Pallas kernels: 73.1 us -> 71.9 us  [shards(): pl.pallas_call(functools.partial(kernel, sizes), out_shape=(jax.ShapeDtyp...]
where the time goes in v4:
time: 75.4 us; the launch traced here: 75.1 us
  Pallas kernels  74.5 us (99%)
    pallas_call x1, Pallas kernels, shards(): pl.pallas_call(functools.partial(kernel, sizes), out_shape=(jax.ShapeDtyp...  71.9 us
    pallas_call x1, Pallas kernels, shards(): pl.pallas_call(finish, out_shape=(jax.ShapeDtypeStruct((layers, rows, wid...  2.57 us

profile of v4, /device:TPU:1, one launch (start us, length us, event | category | flops | bytes accessed | tf_op | source)
XLA Modules:
  0.0 75.1 jit_solution(14440683426502728609)
XLA Ops:
  0.6 71.9 %adjoint_step.1 = (f32[4,16,1024]{2,1,0:T(8,128)}, f32[3,3,4,16,1024]{4,3,2,1,0:T(8,128)}, f32[8,128]{1,0:T(8,128)}) custom-call(s32[2]{0:T(128)} %table.1, f32[4,16,1024]{2,1,0:T(8,128)} %s_hbm.1, f32[4,16,1024]{2,1,0:T(8,128)} %t_hbm.1, f32[4,16,1024]{2,1,0:T(8,128)} %f_hbm.1, bf16[2,3,4,16,1024]{4,3,2,1,0:T(8,128)(2,1)} %m_hbm.1), custom_call_target="tpu_custom_call" | custom-call | tf_op jit(solution)/shard_map/adjoint_step/pallas_call | solution.py:648
  72.6 2.6 %finish.1 = (f32[4,16,1024]{2,1,0:T(8,128)}, f32[3,4,16,1024]{3,2,1,0:T(8,128)}) custom-call(f32[8,128]{1,0:T(8,128)} %get-tuple-element.5.coef_hbm, f32[4,16,1024]{2,1,0:T(8,128)} %get-tuple-element.6.adv_hbm, f32[3,3,4,16,1024]{4,3,2,1,0:T(8,128)} %get-tuple-element.7.zs_hbm), custom_call_target="tpu_custom_call" | custom-call | tf_op jit(solution)/shard_map/finish/pallas_call | solution.py:676

commit v5 on v4

--- a/solution.py
+++ b/solution.py
@@ -45,7 +45,7 @@
 
 def kernel(
     sizes, table, s_hbm, t_hbm, f_hbm, m_hbm, adv_hbm, zs_hbm, coef_ref,
-    s_v, d_v, m_v, T, Q, I, z0, z1, z2, eu0, ed0,
+    s_v, d_v, m_v, T, Q, I, z0, z1, z2, trial, eu0, ed0,
     sub_out, sub_in, dia_out, dia_in, fwd_out, fwd_in, side_out, side_in, mine, plane, column, temp_v,
     load_sem, store_sem, dia_s, dia_r, rad_s, rad_r, sub_s, sub_r, cor_s, cor_r, fwd_s, fwd_r, late_s, late_r, edge_s, edge_r,
     plane_s, plane_r, column_s, column_r, relay,
@@ -404,14 +404,35 @@
 
     def early(L, at):
         across_layers(L, at)
+        across_rows(L, at)
         across_columns(L, at)
 
-    def early_sums(L, at):
-        for c in (0, 2):
-            z1[c, L, at] = column_sum(z0, c, L, at)
+    def early_second(L, at):
+        for c in range(3):
+            total = column_sum(z0, c, L, at)
+            z1[c, L, at] = total
+            trial[c, L, at] = I[L, at] * (total + other_sum(z0, c, L, at))
+
+    def early_third(L, at):
+        for c in range(3):
+            z2[c, L, at] = column_sum(trial, c, L, at)
 
     over_layers(early, 2, inner)
-    over_layers(early_sums, 1, inner)
+    over_layers(early_second, 1, inner)
+    over_layers(early_third, 0, inner, False)
+
+    octet = lax.broadcasted_iota(jnp.int32, (8, full), 0)
+
+    def late_sums(ref, target, c, L, reach):
+        x = ref[c, L]
+        up_rows = (octet >= 4 - reach) & (octet < 4)
+        down_rows = (octet >= 4) & (octet < 4 + reach)
+        tile = jnp.where(up_rows, pltpu.roll(x[8:16], 4, 0), jnp.where(down_rows, pltpu.roll(x[0:8], 4, 0), x[16:24]))
+        total = later(tile, 1) + earlier(tile, 1)
+        moved = pltpu.roll(total, 4, 0)
+        first_tile = jnp.where(octet < reach, moved, target[c, L, 0:8])
+        last_tile = jnp.where(octet >= 8 - reach, moved, target[c, L, 8:16])
+        return jnp.concatenate([first_tile, last_tile, total], 0)
 
     arrived([sub_main[0][1]], has_down)
     arrived([sub_main[1][1]], has_up)
@@ -442,23 +463,31 @@
     across_rows(bottom - 2, high_half)
     across_rows(top + 2, low_half)
 
-    def second(L, at):
+    def second(L, carry):
+        for c in range(3):
+            z1[c, L] = I[L] * (late_sums(z0, z1, c, L, 1) + other_sum(z0, c, L, every))
+        return carry
+
+    def second_deep(L, at):
         for c in (0, 2):
             z1[c, L, at] = I[L, at] * (z1[c, L, at] + other_sum(z0, c, L, at))
         z1[1, L, at] = I[L, at] * (column_sum(z0, 1, L, at) + other_sum(z0, 1, L, at))
 
-    def second_outer(L, at):
-        for c in (0, 2):
-            z1[c, L, at] = I[L, at] * (column_sum(z0, c, L, at) + other_sum(z0, c, L, at))
-        z1[1, L, at] = I[L, at] * (column_sum(z0, 1, L, at) + other_sum(z0, 1, L, at))
-
-    def third(L, at):
+    def third(L, carry):
+        for c in range(3):
+            z2[c, L] = I[L] * (late_sums(z1, z2, c, L, 2) + other_sum(z1, c, L, every))
+        return carry
+
+    def third_deep(L, at):
         for c in range(3):
             z2[c, L, at] = I[L, at] * (column_sum(z1, c, L, at) + other_sum(z1, c, L, at))
 
-    over_layers(second, 1, inner)
-    over_layers(second_outer, 1, outer, False)
-    over_layers(third, 0, every)
+    lax.fori_loop(bottom, top + 1, second, 0)
+    second_deep(bottom - 1, high_half)
+    second_deep(top + 1, low_half)
+    lax.fori_loop(H, H + layers, third, 0)
+    third_deep(bottom, high_half)
+    third_deep(top, low_half)
 
     def folded(x):
         total = jnp.zeros((8, 128), jnp.float32)
@@ -656,7 +685,7 @@
             out_specs=(in_hbm, in_hbm, pl.BlockSpec(memory_space=pltpu.VMEM)),
             scratch_shapes=[
                 block, block, pltpu.VMEM(stored_motions.shape, stored_motions.dtype),
-                field, field, field, vector, vector, vector,
+                field, field, field, vector, vector, vector, vector,
                 pltpu.VMEM((layers + 2, rows, width), f32), pltpu.VMEM((layers + 2, rows, width), f32),
                 pltpu.VMEM((2, layers + 1, 8, long), f32), pltpu.VMEM((2, layers + 1, 8, long), f32),
                 pltpu.VMEM((2, 8, 128), f32), pltpu.VMEM((2, 8, 128), f32),

time: 75.4 us -> 74.7 us (level)
  no operation moved by 1% of the time
where the time goes in v5:
time: 74.7 us; the launch traced here: 74.5 us
  Pallas kernels  73.9 us (99%)
    pallas_call x1, Pallas kernels, shards(): pl.pallas_call(functools.partial(kernel, sizes), out_shape=(jax.ShapeDtyp...  71.3 us
    pallas_call x1, Pallas kernels, shards(): pl.pallas_call(finish, out_shape=(jax.ShapeDtypeStruct((layers, rows, wid...  2.57 us

profile of v5, /device:TPU:1, one launch (start us, length us, event | category | flops | bytes accessed | tf_op | source)
XLA Modules:
  0.0 74.5 jit_solution(8705667451906890797)
XLA Ops:
  0.6 71.3 %adjoint_step.1 = (f32[4,16,1024]{2,1,0:T(8,128)}, f32[3,3,4,16,1024]{4,3,2,1,0:T(8,128)}, f32[8,128]{1,0:T(8,128)}) custom-call(s32[2]{0:T(128)} %table.1, f32[4,16,1024]{2,1,0:T(8,128)} %s_hbm.1, f32[4,16,1024]{2,1,0:T(8,128)} %t_hbm.1, f32[4,16,1024]{2,1,0:T(8,128)} %f_hbm.1, bf16[2,3,4,16,1024]{4,3,2,1,0:T(8,128)(2,1)} %m_hbm.1), custom_call_target="tpu_custom_call" | custom-call | tf_op jit(solution)/shard_map/adjoint_step/pallas_call | solution.py:677
  72.0 2.6 %finish.1 = (f32[4,16,1024]{2,1,0:T(8,128)}, f32[3,4,16,1024]{3,2,1,0:T(8,128)}) custom-call(f32[8,128]{1,0:T(8,128)} %get-tuple-element.5.coef_hbm, f32[4,16,1024]{2,1,0:T(8,128)} %get-tuple-element.6.adv_hbm, f32[3,3,4,16,1024]{4,3,2,1,0:T(8,128)} %get-tuple-element.7.zs_hbm), custom_call_target="tpu_custom_call" | custom-call | tf_op jit(solution)/shard_map/finish/pallas_call | solution.py:705

commit v6 on v5

--- a/solution.py
+++ b/solution.py
@@ -221,7 +221,9 @@
             device_id=device, device_id_type=MESH,
         )
 
-    chunks = (pl.ds(0, width // 2), pl.ds(width // 2, width // 2))
+    n_chunks = 4 if width % 512 == 0 else 2
+    wide = width // n_chunks
+    chunks = [pl.ds(j * wide, wide) for j in range(n_chunks)]
     sub_main = [
         [
             send(sub_out.at[i, pl.ds(0, layers), :, at], sub_in.at[i, pl.ds(0, layers), :, at], sub_s.at[i, j], sub_r.at[i, j], to)
@@ -269,7 +271,7 @@
         [send(ed0.at[layers], ed0.at[0], edge_s.at[2], edge_r.at[2], above)],
         [send(eu0.at[1], eu0.at[layers + 1], edge_s.at[3], edge_r.at[3], below)],
     ]
-    parts = (pl.ds(0, width // 2), pl.ds(width // 2, full - width // 2))
+    parts = chunks[:-1] + [pl.ds(width - wide, wide + 128)]
     rad_rows = [
         [
             send(fwd_out.at[i, :, :, at], fwd_in.at[i, :, :, at], late_s.at[i, j], late_r.at[i, j], to)
@@ -314,7 +316,7 @@
             for copy in copies:
                 copy.wait_send()
 
-    for j in range(2):
+    for j in range(n_chunks):
         start([sub_main[0][j]], has_up)
         start([sub_main[1][j]], has_down)
     for copy in dia_copies:
@@ -393,10 +395,16 @@
         start([rad_rows[0][j]], has_above)
         start([rad_rows[1][j]], has_below)
 
-    arrived([sub_main[0][0]], has_down)
-    arrived([sub_main[1][0]], has_up)
-    unpack(slice(0, width // 2))
-    forward(slice(0, width // 2), 0)
+    def take(j, forwarded=True):
+        columns = slice(j * wide, (j + 1) * wide)
+        arrived([sub_main[0][j]], has_down)
+        arrived([sub_main[1][j]], has_up)
+        unpack(columns)
+        if forwarded:
+            forward(columns, j)
+
+    for j in range(n_chunks // 2):
+        take(j)
 
     for group in (rad_main, rad_deep, rad_side):
         arrived(group[0], has_below)
@@ -434,16 +442,15 @@
         last_tile = jnp.where(octet >= 8 - reach, moved, target[c, L, 8:16])
         return jnp.concatenate([first_tile, last_tile, total], 0)
 
-    arrived([sub_main[0][1]], has_down)
-    arrived([sub_main[1][1]], has_up)
-    unpack(slice(width // 2, width))
+    for j in range(n_chunks // 2, n_chunks):
+        take(j, j < n_chunks - 1)
     arrived([sub_side[0]], has_down)
     arrived([sub_side[1]], has_up)
     for way in range(2):
         for k in range(layers - 1):
             sub_in[way, k, :, side] = pltpu.roll(side_in[way], (-8 * k) % 128, 1)
     unpack(side)
-    forward(slice(width // 2, full), 1)
+    forward(slice(width - wide, full), n_chunks - 1)
 
     def late(L, carry):
         across_layers(L, outer)
@@ -604,31 +611,7 @@
     copies.wait_recv()
     copies.wait_send()
     row = jnp.sum(column[...], axis=0)
-    m0, m1, m2, m3, m4, m5 = (
-        jnp.sum(jnp.where(tile_lane == j, row, 0.0), axis=1, keepdims=True) for j in range(6)
-    )
-
-    def step(p):
-        a, b, c = p
-        square = (a * a, 2.0 * a * b, b * b + 2.0 * a * c, 2.0 * b * c, c * c)
-        energy = sum(x * m for x, m in zip(square, (m0, m1, m2, m3, m4)))
-        moved = sum(x * m for x, m in zip(square, (m1, m2, m3, m4, m5)))
-        return jnp.clip(energy / (energy - moved), ALPHA_LOW, ALPHA_HIGH)
-
-    one, none = jnp.ones_like(m0), jnp.zeros_like(m0)
-    p0 = (one, none, none)
-    alpha0 = step(p0)
-    p1 = (1.0 - alpha0, alpha0, none)
-    alpha1 = step(p1)
-    p2 = (p1[0] * (1.0 - alpha1), p1[1] * (1.0 - alpha1) + p1[0] * alpha1, p1[1] * alpha1)
-    alpha2 = step(p2)
-    c0, c1, c2 = (alpha0 * x + alpha1 * y + alpha2 * w for x, y, w in zip(p0, p1, p2))
-
-    wide = jnp.zeros((8, 128), jnp.float32)
-    row_of = lax.broadcasted_iota(jnp.int32, (8, 128), 0)
-    for n, value in enumerate((c0, c1, c2)):
-        wide = jnp.where(row_of == n, value, wide)
-    coef_ref[...] = wide
+    coef_ref[...] = jnp.broadcast_to(row, (8, 128))
 
 
 def finish(coef_hbm, adv_hbm, zs_hbm, temp_hbm, vel_hbm, coef, adv, zs, temp, vel, load_sem, store_sem):
@@ -643,7 +626,26 @@
         loads[-2].start()
         loads[-1].start()
     loads[0].wait()
-    c0, c1, c2 = (coef[n : n + 1, 0:1] for n in range(3))
+    row, lane = coef[0:1], lax.broadcasted_iota(jnp.int32, (1, 128), 1)
+    m0, m1, m2, m3, m4, m5 = (
+        jnp.sum(jnp.where(lane == j, row, 0.0), axis=1, keepdims=True) for j in range(6)
+    )
+
+    def step(p):
+        a, b, c = p
+        square = (a * a, 2.0 * a * b, b * b + 2.0 * a * c, 2.0 * b * c, c * c)
+        energy = sum(x * m for x, m in zip(square, (m0, m1, m2, m3, m4)))
+        moved = sum(x * m for x, m in zip(square, (m1, m2, m3, m4, m5)))
+        return jnp.clip(energy / (energy - moved), ALPHA_LOW, ALPHA_HIGH)
+
+    one, none = jnp.ones_like(m0), jnp.zeros_like(m0)
+    p0 = (one, none, none)
+    alpha0 = step(p0)
+    p1 = (1.0 - alpha0, alpha0, none)
+    alpha1 = step(p1)
+    p2 = (p1[0] * (1.0 - alpha1), p1[1] * (1.0 - alpha1) + p1[0] * alpha1, p1[1] * alpha1)
+    alpha2 = step(p2)
+    c0, c1, c2 = (alpha0 * x + alpha1 * y + alpha2 * w for x, y, w in zip(p0, p1, p2))
     for l in range(layers):
         loads[2 * l + 1].wait()
         loads[2 * l + 2].wait()
@@ -693,8 +695,8 @@
                 pltpu.VMEM((2, 8, 128), f32), pltpu.VMEM((2, 8, 128), f32), pltpu.VMEM((2, 1, 128), f32), pltpu.VMEM((n_g, 1, 128), f32), pltpu.VMEM((n_z, 1, 128), f32),
                 block,
                 dma((4,)), dma((4,)), dma((2,)), dma((2,)), dma((2, 2, 3)), dma((2, 2, 3)),
-                dma((2, 2)), dma((2, 2)), dma((2,)), dma((2,)), dma((2, 3)), dma((2, 3)),
-                dma((2, 2)), dma((2, 2)), dma((4,)), dma((4,)),
+                dma((2, 4)), dma((2, 4)), dma((2,)), dma((2,)), dma((2, 3)), dma((2, 3)),
+                dma((2, 4)), dma((2, 4)), dma((4,)), dma((4,)),
                 dma, dma, dma, dma, pltpu.SemaphoreType.REGULAR,
             ],
             compiler_params=pltpu.CompilerParams(

time: 74.7 us -> 74.6 us (level)
  no operation moved by 1% of the time
where the time goes in v6:
time: 74.6 us; the launch traced here: 74.4 us
  Pallas kernels  73.7 us (99%)
    pallas_call x1, Pallas kernels, shards(): pl.pallas_call(functools.partial(kernel, sizes), out_shape=(jax.ShapeDtyp...  71.2 us
    pallas_call x1, Pallas kernels, shards(): pl.pallas_call(finish, out_shape=(jax.ShapeDtypeStruct((layers, rows, wid...  2.57 us

profile of v6, /device:TPU:1, one launch (start us, length us, event | category | flops | bytes accessed | tf_op | source)
XLA Modules:
  0.0 74.4 jit_solution(16442144267664967695)
XLA Ops:
  0.6 71.2 %adjoint_step.1 = (f32[4,16,1024]{2,1,0:T(8,128)}, f32[3,3,4,16,1024]{4,3,2,1,0:T(8,128)}, f32[8,128]{1,0:T(8,128)}) custom-call(s32[2]{0:T(128)} %table.1, f32[4,16,1024]{2,1,0:T(8,128)} %s_hbm.1, f32[4,16,1024]{2,1,0:T(8,128)} %t_hbm.1, f32[4,16,1024]{2,1,0:T(8,128)} %f_hbm.1, bf16[2,3,4,16,1024]{4,3,2,1,0:T(8,128)(2,1)} %m_hbm.1), custom_call_target="tpu_custom_call" | custom-call | tf_op jit(solution)/shard_map/adjoint_step/pallas_call | solution.py:679
  71.8 2.6 %finish.1 = (f32[4,16,1024]{2,1,0:T(8,128)}, f32[3,4,16,1024]{3,2,1,0:T(8,128)}) custom-call(f32[8,128]{1,0:T(8,128)} %get-tuple-element.5.coef_hbm, f32[4,16,1024]{2,1,0:T(8,128)} %get-tuple-element.6.adv_hbm, f32[3,3,4,16,1024]{4,3,2,1,0:T(8,128)} %get-tuple-element.7.zs_hbm), custom_call_target="tpu_custom_call" | custom-call | tf_op jit(solution)/shard_map/finish/pallas_call | solution.py:707
